TPU v7x, 256 devices: a whole 4x4x8 slice. The times are simulated.
256 devices in a mesh: sep: 16 (over z, core), tile: 16 (over x, y).
Axes of the slice: x: 4, y: 4, z: 8, core: 2. Of those that a mesh axis runs over, the one named last changes fastest.
Arguments:
- first_frame: float32 [2560, 2560], P('tile'), may hold values from -6 to 6
- second_frames: float32 [16, 2560, 2560], P('sep', 'tile'), may hold values from -6 to 6
- shifts: int32 [2, 16, 80, 80], P(None, 'sep', 'tile'), may hold values from -8 to 8
- fractions: float32 [2, 16, 80, 80], P(None, 'sep', 'tile'), may hold values from 0 to 1
Outputs:
- product_planes: float32 [80, 80, 1024], P('tile', 'sep')
All inputs are finite; a program needn't handle non-finite values.
Results may differ from a plain program's by a relative error of at most 0.0003.
Values sent between devices are 32-bit elements; how exact they have to be, the bound alone decides.
No kernel may reach another device: no remote copies, remote signals or barrier semaphores. Data moves between devices by JAX's collectives and lax.ppermute only.
A program may use at most 128 MiB of HBM per device.

v0:
```python
import math

import jax
import jax.numpy as jnp
from jax import lax
from jax.sharding import PartitionSpec as P

WIN = 32
MAXSHIFT = 8
HALO = 16


epsilon = 1e-06
highest = lax.Precision.HIGHEST


def extended(cells, sides, width):
    for axis, dim in sides:
        count = lax.axis_size(axis)
        ends = count - 1
        head = lax.slice_in_dim(cells, 0, width, axis=dim)
        tail = lax.slice_in_dim(cells, cells.shape[dim] - width, cells.shape[dim], axis=dim)
        cells = jnp.concatenate(
            [
                lax.ppermute(tail, axis, [(i, (i + 1) % count) for i in range(ends)]),
                cells,
                lax.ppermute(head, axis, [((i + 1) % count, i) for i in range(ends)]),
            ],
            axis=dim,
        )
    return cells


def joined(array, axis, combine):
    everything = lax.all_gather(array, axis)
    first = everything[0]

    def lap(k, so_far):
        return combine(so_far, everything[k])

    return lax.fori_loop(1, lax.axis_size(axis), lap, first)


def cubic_weights(fraction):
    squared = fraction * fraction
    cubed = squared * fraction
    return jnp.stack(
        [
            -0.5 * cubed + squared - 0.5 * fraction,
            1.5 * cubed - 2.5 * squared + 1.0,
            -1.5 * cubed + 2.0 * squared + 0.5 * fraction,
            0.5 * cubed - 0.5 * squared,
        ],
        axis=-1,
    )


def tap_matrix(taps, offsets, reach):
    inner = jnp.arange(WIN, dtype=jnp.int32)
    outer = jnp.arange(reach, dtype=jnp.int32)
    target = outer[None, :] - inner[:, None]
    lifted = offsets[..., None, None] + MAXSHIFT
    total = jnp.zeros(offsets.shape + (WIN, reach), jnp.float32)
    for tap_index in range(4):
        hit = (target == lifted + tap_index).astype(jnp.float32)
        total = total + taps[..., tap_index][..., None, None] * hit
    return total


def dft_tables():
    indices = jnp.arange(WIN, dtype=jnp.int32)
    phases = indices[:, None] * indices[None, :] % WIN
    angles = phases.astype(jnp.float32) * (2.0 * math.pi / WIN)
    return (jnp.cos(angles), jnp.sin(angles))


def along_cols(field, table):
    return jnp.einsum("rcx,cd->rdx", field, table, precision=highest)


def along_rows(table, field):
    return jnp.einsum("kr,rdx->kdx", table, field, precision=highest)


def forward(field, cos_table, sine_table):
    col_re = along_cols(field, cos_table)
    col_im = -along_cols(field, sine_table)
    out_re = along_rows(cos_table, col_re) + along_rows(sine_table, col_im)
    out_im = along_rows(cos_table, col_im) - along_rows(sine_table, col_re)
    return (out_re, out_im)


def inverse_real(prod_re, prod_im, cos_table, sine_table):
    mid_re = along_cols(prod_re, cos_table) - along_cols(prod_im, sine_table)
    mid_im = along_cols(prod_re, sine_table) + along_cols(prod_im, cos_table)
    return along_rows(cos_table, mid_re) - along_rows(sine_table, mid_im)


def multiply(left, right):
    return left * right


def local(first_frame, second_frames, shifts, fractions):
    pair_count, band_rows, frame_cols = second_frames.shape
    win_rows = band_rows // WIN
    win_cols = frame_cols // WIN
    windows = win_rows * win_cols
    reach = WIN + 2 * MAXSHIFT + 3
    extra = reach - WIN
    lead = HALO - MAXSHIFT - 1
    cos_table, sine_table = dft_tables()
    first_win = (
        first_frame.reshape(win_rows, WIN, win_cols, WIN)
        .transpose(1, 3, 0, 2)
        .reshape(WIN, WIN, windows)
    )
    first_win = first_win - jnp.mean(first_win, axis=(0, 1), keepdims=True)
    first_pow = jnp.mean(first_win * first_win, axis=(0, 1))
    first_re, first_im = forward(first_win, cos_table, sine_table)
    padded = extended(second_frames, (("tile", 1),), HALO)
    padded = jnp.pad(padded, ((0, 0), (0, WIN), (HALO, HALO + WIN)))
    main_rows = padded[:, lead : lead + band_rows].reshape(pair_count, win_rows, WIN, -1)
    next_rows = padded[:, lead + WIN : lead + WIN + band_rows].reshape(
        pair_count, win_rows, WIN, -1
    )[:, :, :extra]
    row_blocks = jnp.concatenate([main_rows, next_rows], axis=2)
    main_cols = row_blocks[..., lead : lead + frame_cols].reshape(
        pair_count, win_rows, reach, win_cols, WIN
    )
    next_cols = row_blocks[..., lead + WIN : lead + WIN + frame_cols].reshape(
        pair_count, win_rows, reach, win_cols, WIN
    )[..., :extra]
    regions = jnp.concatenate([main_cols, next_cols], axis=4)
    row_matrix = tap_matrix(cubic_weights(fractions[0]), shifts[0], reach)
    col_matrix = tap_matrix(cubic_weights(fractions[1]), shifts[1], reach)
    row_mix = jnp.einsum("pijru,piujv->pijrv", row_matrix, regions, precision=highest)
    deformed = jnp.einsum("pijrv,pijcv->rcpij", row_mix, col_matrix, precision=highest)
    second_win = deformed.reshape(WIN, WIN, pair_count * windows)
    second_win = second_win - jnp.mean(second_win, axis=(0, 1), keepdims=True)
    second_pow = jnp.mean(second_win * second_win, axis=(0, 1)).reshape(pair_count, windows)
    second_re, second_im = forward(second_win, cos_table, sine_table)
    second_re = second_re.reshape(WIN, WIN, pair_count, windows)
    second_im = second_im.reshape(WIN, WIN, pair_count, windows)
    prod_re = first_re[:, :, None, :] * second_re + first_im[:, :, None, :] * second_im
    prod_im = first_re[:, :, None, :] * second_im - first_im[:, :, None, :] * second_re
    corr = inverse_real(
        prod_re.reshape(WIN, WIN, -1), prod_im.reshape(WIN, WIN, -1), cos_table, sine_table
    )
    corr = corr.reshape(WIN, WIN, pair_count, windows)
    scaling = 1.0 / (
        WIN * WIN * WIN * WIN * jnp.sqrt((first_pow[None, :] + epsilon) * (second_pow + epsilon))
    )
    planes = 1.0 + corr * scaling[None, None]
    planes = planes.reshape(WIN * WIN, pair_count, win_rows, win_cols).transpose(1, 2, 3, 0)
    local_prod = jnp.prod(planes, axis=0)
    merged = joined(local_prod, "sep", multiply)
    block_cols = win_cols // lax.axis_size("sep")
    return lax.dynamic_slice_in_dim(merged, lax.axis_index("sep") * block_cols, block_cols, 1)


def solution(mesh):
    in_specs = (
        P("tile", None),
        P("sep", "tile", None),
        P(None, "sep", "tile", None),
        P(None, "sep", "tile", None),
    )
    out_specs = P("tile", "sep", None)
    return jax.shard_map(local, mesh=mesh, in_specs=in_specs, out_specs=out_specs, check_vma=False)
```

profile of v0, /device:TPU:6, one launch (start us, length us, event | category | flops | bytes accessed | tf_op | source)
XLA Modules:
  0.0 399.2 jit_solution(5951126583401985583)
XLA Ops:
  6.5 1.0 fusion.260
  7.6 3.5 collective-permute-start
  11.0 4.5 %collective-permute-start.1 = (f32[1,16,2560]{2,1,0:T(8,128)S(1)}, f32[1,16,2560]{2,1,0:T(8,128)S(1)}, u32[]{:S(2)}, u32[]{:S(2)}) collective-permute-start(f32[1,16,2560]{2,1,0:T(8,128)S(1)} %get-tuple-element.110), channel_id=1, source_target_pairs={{1,0},{2,1},{3,2},{4,3},{5,4},{6,5},{7,6},{8,7},{9,8},{10,9},{11,1... | collective-permute-start | bytes 491528 | tf_op jit(solution)/shard_map/ppermute | solution.py:27
  15.5 5.1 %reshape.416 = f32[5,32,80,32]{3,2,1,0:T(8,128)} reshape(f32[160,2560]{1,0:T(8,128)} %param.6) | data formatting | bytes 3276800 | tf_op jit(solution)/shard_map/reshape | solution.py:113
  20.6 3.5 bitcast_reduce_fusion.1
  24.1 1.2 copy-done
  25.3 1.0 multiply_reduce_fusion
  26.4 6.7 %copy.40 = f32[32,32,5,80]{3,2,1,0:T(8,128)} copy(f32[32,32,5,80]{1,3,0,2:T(8,128)} %bitcast.164) | data formatting | bytes 3276800 | tf_op jit(solution)/shard_map/transpose | solution.py:114
  33.2 3.6 reshape.417
  36.7 2.0 negate_bitcast_fusion.1
  38.7 2.0 fusion.87
  40.7 3.0 fusion.73
  43.8 4.3 %fusion.71 = f32[32,32,400]{2,0,1:T(8,128)} fusion(f32[32,32,400]{2,1,0:T(8,128)S(1)} %negate_bitcast_fusion.1), kind=kOutput, calls=%fused_computation.91 | convolution fusion | flops 157300736 | bytes 3276800 | tf_op jit(solution)/shard_map/kr,rdx->kdx/dot_general | solution.py:82
  48.2 5.0 %fusion.97 = f32[32,32,400]{2,0,1:T(8,128)} fusion(f32[32,32,400]{2,0,1:T(8,128)S(1)} %fusion.73, f32[32,32,400]{2,1,0:T(8,128)S(1)} %fusion.87), kind=kOutput, calls=%fused_computation.110 | convolution fusion | flops 157710336 | bytes 4915200 | tf_op jit(solution)/shard_map/kr,rdx->kdx/dot_general | solution.py:82
  53.2 0.6 select_maximum_fusion
  53.8 0.2 fusion.259
  54.1 2.9 reshape.419
  57.0 2.3 slice.54
  59.3 2.9 reshape.418
  62.1 16.8 %fusion.48 = (f32[1,5,51,2560]{3,0,2,1:T(1,128)S(1)}, f32[1,5,51,2560]{3,0,2,1:T(1,128)}) fusion(f32[1,5,32,2624]{3,0,2,1:T(1,128)} %reshape.418, f32[1,5,19,2624]{3,0,2,1:T(1,128)} %slice.54), kind=kLoop, calls=%fused_computation.57 | loop fusion | flops 1305600 | bytes 7898880 | tf_op jit(solution)/shard_map/concatenate | solution.py:126
  79.0 8.6 %copy.47 = f32[1,5,51,2560]{2,3,1,0:T(8,128)} copy(f32[1,5,51,2560]{3,0,2,1:T(1,128)} %get-tuple-element.106) | data formatting | bytes 5222400 | tf_op jit(solution)/shard_map/slice | solution.py:130
  87.5 4.9 %slice.57 = f32[1,5,51,80,19]{2,4,3,1,0:T(8,128)} slice(f32[1,5,51,80,32]{2,4,3,1,0:T(8,128)} %bitcast.167), slice={[0:1], [0:5], [0:51], [0:80], [0:19]} | slice | bytes 3100800 | tf_op jit(solution)/shard_map/slice | solution.py:130
  92.5 9.3 %copy.97 = f32[1,5,51,80,19]{4,2,3,1,0:T(8,128)} copy(f32[1,5,51,80,19]{2,4,3,1,0:T(8,128)} %slice.57) | data formatting | bytes 3100800
  101.7 6.0 %copy.46 = f32[1,5,51,2560]{2,3,1,0:T(8,128)} copy(f32[1,5,51,2560]{3,0,2,1:T(1,128)S(1)} %get-tuple-element.105) | data formatting | bytes 5222400 | tf_op jit(solution)/shard_map/slice | solution.py:127
  107.8 10.2 %copy.49 = f32[1,5,51,80,32]{4,2,3,1,0:T(8,128)} copy(f32[1,5,51,80,32]{2,4,3,1,0:T(8,128)} %bitcast.166) | data formatting | bytes 5222400 | tf_op jit(solution)/shard_map/reshape | solution.py:127
  118.0 19.8 %fusion = f32[5,80,32,51]{3,2,1,0:T(8,128)S(1)} fusion(f32[1,5,51,80,19]{4,2,3,1,0:T(8,128)} %copy.97, f32[1,5,51,80,32]{4,2,3,1,0:T(8,128)} %copy.49, f32[5,80]{1,0:T(8,128)S(1)} %get-tuple-element.132, s32[5,80]{1,0:T(8,128)S(1)} %get-tuple-element.135, f32[5,80]{1,0:T(8,128)S(1)} %get-tuple-element.133, s32[5,80]{1,0:T(8,128)S(1)} %get-tuple-element.136, ...), kind=kOutput, calls=%fused_computation.2 | convolution fusion | flops 407734784 | bytes 6792128 | tf_op jit(solution)/shard_map/pijru,piujv->pijrv/dot_general | solution.py:136
  137.7 18.8 %bitcast_reduce_fusion = (f32[5,80]{1,0:T(8,128)S(1)}, f32[5,80,32,32]{3,2,1,0:T(8,128)}) fusion(f32[5,80,32,51]{3,2,1,0:T(8,128)S(1)} %fusion, f32[5,80]{1,0:T(8,128)S(1)} %get-tuple-element.122, s32[5,80]{1,0:T(8,128)S(1)} %get-tuple-element.139, f32[5,80]{1,0:T(8,128)S(1)} %get-tuple-element.123, s32[5,80]{1,0:T(8,128)S(1)} %get-tuple-element.140, ...), kind=kOutput, calls=%fused_computation.5 | convolution fusion | flops 258265200 | bytes 4270528 | tf_op jit(solution)/shard_map/pijrv,pijcv->rcpij/dot_general | solution.py:137
  156.6 7.9 %fusion.4 = f32[5,80]{1,0:T(8,128)S(1)} fusion(f32[5,80,32,32]{3,2,1,0:T(8,128)} %get-tuple-element.130, f32[5,80]{1,0:T(8,128)S(1)} %broadcast_multiply_fusion), kind=kLoop, calls=%fused_computation.8 | loop fusion | flops 1228400 | bytes 1641600 | tf_op jit(solution)/shard_map/reduce_sum | solution.py:140
  164.5 5.5 %copy.50 = f32[32,32,400]{2,1,0:T(8,128)S(1)} copy(f32[32,32,400]{0,1,2:T(8,128)} %bitcast.165) | data formatting | bytes 3276800 | tf_op jit(solution)/shard_map/reshape | solution.py:138
  170.0 2.0 fusion.92
  172.0 2.0 negate_bitcast_fusion
  174.0 3.0 fusion.65
  177.0 3.0 fusion.63
  180.0 3.3 fusion.103
  183.3 3.0 fusion.106
  186.4 3.5 multiply_add_fusion.1
  189.8 4.4 %fusion.57 = f32[32,32,400]{2,0,1:T(8,128)} fusion(f32[32,32,400]{2,0,1:T(8,128)S(1)} %get-tuple-element.104), kind=kOutput, calls=%fused_computation.77 | convolution fusion | flops 157300736 | bytes 3276800 | tf_op jit(solution)/shard_map/rcx,cd->rdx/dot_general | solution.py:78
  194.2 4.8 %fusion.55 = f32[32,32,400]{2,0,1:T(8,128)} fusion(f32[32,32,400]{2,0,1:T(8,128)S(1)} %get-tuple-element.104), kind=kOutput, calls=%fused_computation.75 | convolution fusion | flops 157300736 | bytes 3276800 | tf_op jit(solution)/shard_map/rcx,cd->rdx/dot_general | solution.py:78
  199.1 4.9 %subtract_bitcast_fusion = f32[32,32,400]{2,1,0:T(8,128)S(1)} fusion(f32[32,32,400]{2,0,1:T(8,128)} %fusion.57, f32[32,32,400]{2,0,1:T(8,128)S(1)} %get-tuple-element.103), kind=kOutput, calls=%fused_computation.70 | convolution fusion | flops 157710336 | bytes 4915200 | tf_op jit(solution)/shard_map/rcx,cd->rdx/dot_general | solution.py:78
  204.0 3.1 add_bitcast_fusion
  207.1 3.0 fusion.51
  210.1 3.4 multiply_add_fusion
  213.5 1.2 copy.69
  214.7 2.6 reshape.424
  217.3 3.6 copy.70
  220.9 140.8 %all-gather.2.cloned.1.call-done = f32[16,5,80,1024]{3,2,1,0:T(8,128)} async-done(((f32[1,5,80,1024]{3,2,1,0:T(8,128)}), f32[16,5,80,1024]{3,2,1,0:T(8,128)}) %all-gather.2.cloned.1.call-update) | async-done | bytes 26214416 | tf_op jit(solution)/shard_map/all_gather | solution.py:35
  361.7 1.5 slice_bitcast_fusion
  363.3 28.2 %while.15 = (s32[]{:T(128)}, f32[5,80,1024]{2,1,0:T(8,128)S(1)}, f32[16,5,80,1024]{3,2,1,0:T(8,128)}, s32[]{:T(128)}, s32[]{:T(128)}, /*index=5*/s32[]{:T(128)}) while((s32[]{:T(128)}, f32[5,80,1024]{2,1,0:T(8,128)S(1)}, f32[16,5,80,1024]{3,2,1,0:T(8,128)}, s32[]{:T(128)}, s32[]{:T(128)}, /*index=5*/s32[]{:T(128)}) %tuple.64), condition=%wide.region_5.6_spmd, body=%wide.region_4.5_spmd.sunk | while | flops 409605 | bytes 4915315 | solution.py:41
  363.3 1.9 bitcast_multiply_fusion.3
  365.2 1.9 bitcast_multiply_fusion.3
  367.0 1.9 bitcast_multiply_fusion.3
  368.9 1.9 bitcast_multiply_fusion.3
  370.8 1.9 bitcast_multiply_fusion.3
  372.7 1.9 bitcast_multiply_fusion.3
  374.6 1.9 bitcast_multiply_fusion.3
  376.4 1.9 bitcast_multiply_fusion.3
  378.3 1.9 bitcast_multiply_fusion.3
  380.2 1.9 bitcast_multiply_fusion.3
  382.1 1.9 bitcast_multiply_fusion.3
  384.0 1.9 bitcast_multiply_fusion.3
  385.9 1.9 bitcast_multiply_fusion.3
  387.7 1.9 bitcast_multiply_fusion.3
  389.6 1.9 bitcast_multiply_fusion.3
  391.5 0.7 constant_dynamic-slice_fusion
  (35 shorter events, 0.4 us)
Async XLA Ops:
  6.5 355.2 %all-gather.2.cloned.1.call-start = ((), (), s32[]{:S(2)}) async-start(), calls=%async_computation | async-start | bytes 27852800 | tf_op jit(solution)/shard_map/all_gather | solution.py:35
  7.6 45.7 %collective-permute-start = (f32[1,16,2560]{2,1,0:T(8,128)S(1)}, f32[1,16,2560]{2,1,0:T(8,128)S(1)}, u32[]{:S(2)}, u32[]{:S(2)}) collective-permute-start(f32[1,16,2560]{2,1,0:T(8,128)S(1)} %get-tuple-element.109), channel_id=1, source_target_pairs={{0,1},{1,2},{2,3},{3,4},{4,5},{5,6},{6,7},{7,8},{8,9},{9,10},{10,1... | collective-permute-start | bytes 491528 | tf_op jit(solution)/shard_map/ppermute | solution.py:25
  11.0 42.2 %collective-permute-start.1 = (f32[1,16,2560]{2,1,0:T(8,128)S(1)}, f32[1,16,2560]{2,1,0:T(8,128)S(1)}, u32[]{:S(2)}, u32[]{:S(2)}) collective-permute-start(f32[1,16,2560]{2,1,0:T(8,128)S(1)} %get-tuple-element.110), channel_id=1, source_target_pairs={{1,0},{2,1},{3,2},{4,3},{5,4},{6,5},{7,6},{8,7},{9,8},{10,9},{11,1... | collective-permute-start | bytes 491528 | tf_op jit(solution)/shard_map/ppermute | solution.py:27
  20.6 4.7 %copy-start = (f32[5,32,80,32]{3,2,1,0:T(8,128)S(1)}, f32[5,32,80,32]{3,2,1,0:T(8,128)}, u32[]{:S(2)}) copy-start(f32[5,32,80,32]{3,2,1,0:T(8,128)} %reshape.416) | copy-start | bytes 4915204
  40.7 7.5 %copy-start.1 = (f32[32,32,400]{2,1,0:T(8,128)}, f32[32,32,400]{2,1,0:T(8,128)S(1)}, u32[]{:S(2)}) copy-start(f32[32,32,400]{2,1,0:T(8,128)S(1)} %fusion.87) | copy-start | bytes 4915204
  43.7 4.4 %copy-start.8 = (s32[2,1,5,80]{3,1,2,0:T(1,128)S(1)}, s32[2,1,5,80]{3,1,2,0:T(1,128)}, u32[]{:S(2)}) copy-start(s32[2,1,5,80]{3,1,2,0:T(1,128)} %param.8) | copy-start | bytes 9604
  43.8 4.4 %copy-start.7 = (f32[2,1,5,80]{3,1,2,0:T(1,128)S(1)}, f32[2,1,5,80]{3,1,2,0:T(1,128)}, u32[]{:S(2)}) copy-start(f32[2,1,5,80]{3,1,2,0:T(1,128)} %param.9) | copy-start | bytes 9604
  48.2 5.0 %copy-start.6 = (f32[1,160,2560]{2,1,0:T(8,128)S(1)}, f32[1,160,2560]{2,1,0:T(8,128)}, u32[]{:S(2)}) copy-start(f32[1,160,2560]{2,1,0:T(8,128)} %param.7) | copy-start | bytes 4915204
  183.3 3.1 copy-start.2
  183.3 3.1 copy-start.3
  183.3 3.1 copy-start.4
  199.1 4.9 %copy-start.5 = (f32[32,32,400]{2,0,1:T(8,128)S(1)}, f32[32,32,400]{2,0,1:T(8,128)}, u32[]{:S(2)}) copy-start(f32[32,32,400]{2,0,1:T(8,128)} %fusion.55) | copy-start | bytes 4915204
Sparse Core Ops, SparseCore 0:
  221.0 140.6 all-gather.1
where the time goes:
time: 405 us; the launch traced here: 399 us
  waiting for transfers between devices  141 us (35%)
  matrix products  98.1 us (24%)
  local copies, waits for them, and re-layouts  80.3 us (20%)
  other arithmetic  57.7 us (14%)
  between operations  13.9 us (3%)
  starting transfers between devices  7.95 us (2%)
    all_gather x1, waiting for transfers between devices, joined(): everything = lax.all_gather(array, axis)  141 us
    dot_general x10, matrix products, along_rows(): return jnp.einsum('kr,rdx->kdx', table, field, precision=highest)  34.5 us
    mul x15, other arithmetic, multiply(): return left * right  27.9 us
    dot_general x8, matrix products, along_cols(): return jnp.einsum('rcx,cd->rdx', field, table, precision=highest)  25.1 us
    dot_general x1, matrix products, local(): jnp.einsum('pijru,piujv->pijrv', row_matrix, regions, precision=highest)  19.8 us
    dot_general x1, matrix products, local(): jnp.einsum('pijrv,pijcv->rcpij', row_mix, col_matrix, precision=highest)  18.8 us
    concatenate x1, other arithmetic, local(): row_blocks = jnp.concatenate([main_rows, next_rows], axis=2)  16.8 us
    slice x2, local copies, waits for them, and re-layouts, local(): row_blocks[..., lead + WIN:lead + WIN + frame_cols]  13.5 us
  transfers between devices with their start and end apart: 3, of which 1 were waited for; matrix products, arithmetic and copies ran while one was open for 9% of the time, Pallas kernels for 0%

commit v1 on v0

v1 whole, which is shorter than its diff:
```python
import functools
import math

import jax
import jax.numpy as jnp
import ml_dtypes
import numpy as np
from jax import lax
from jax.experimental import pallas as pl
from jax.experimental.pallas import tpu as pltpu
from jax.sharding import PartitionSpec as P

WIN = 32
HALO = 16
EPS = 1e-06
LANES = 128
BLOCKS = 16
ROOT_HALF = math.sqrt(0.5)


def split_table(table):
    high = table.astype(ml_dtypes.bfloat16)
    low = (table - high.astype(np.float64)).astype(ml_dtypes.bfloat16)
    return high, low


def dft_tables():
    major, minor = np.divmod(np.arange(LANES), WIN)
    forward, backward = [], []
    for unit in (0, 4, 1, 2, 3):
        phase = (np.outer(major, unit + 8 * major) + np.outer(minor, minor)) % WIN
        cos = np.cos(phase * (2.0 * np.pi / WIN))
        sin = np.sin(phase * (2.0 * np.pi / WIN))
        if unit in (0, 4):
            half = np.concatenate([cos, -sin], axis=1)
            forward.append((np.concatenate([half, half]), np.concatenate([half, 0 * half])))
            backward.append(np.concatenate([cos.T, -sin.T]))
        else:
            whole = np.block([[cos, -sin], [sin, cos]])
            forward.append((whole, whole))
            backward.append(2.0 * np.block([[cos.T, sin.T], [-sin.T, cos.T]]))
    fwd_hi = np.stack([split_table(a)[0] for a, _ in forward])
    fwd_lo = np.stack([split_table(b)[1] for _, b in forward])
    ends_hi, ends_lo = split_table(np.stack(backward[:2]))
    mids_hi, mids_lo = split_table(np.stack(backward[2:]))
    return fwd_hi, fwd_lo, ends_hi, ends_lo, mids_hi, mids_lo


def split(value):
    high = value.astype(jnp.bfloat16)
    return high, (value - high.astype(jnp.float32)).astype(jnp.bfloat16)


def dot(left, right):
    return jnp.dot(left, right, preferred_element_type=jnp.float32)


def band_kernel(
    win_rows, slab, tall, shift_ref, taps_ref, first_ref, second_ref, *refs
):
    if tall:
        top_ref, bottom_ref, *refs = refs
    (fwd_hi, fwd_lo, ends_hi, ends_lo, mids_hi, mids_lo, out_ref,
     frame, first, second_win, first_win, pair_ends, pair_hi, pair_lo, powers, back) = refs
    count = len(win_rows)
    block = 5 * count
    windows = BLOCKS * block
    frame_rows = frame.shape[1]
    tiles = second_ref.shape[1] // LANES
    lane = lax.broadcasted_iota(jnp.int32, (8, LANES), 1)
    low_half = lane < 64
    mid_half = (lane >= 32) & (lane < 96)
    even = (lane % 64) < 32

    def rows_of(ref, top, bottom, g):
        cols = slice(g * LANES, (g + 1) * LANES)
        if not tall:
            return ref[16:144, cols]
        return jnp.concatenate([top[:, cols], ref[0:48, cols], ref[112:160, cols], bottom[:, cols]], axis=0)

    wide = lax.broadcasted_iota(jnp.int32, (frame_rows, LANES), 1) < 64
    before = jnp.zeros((frame_rows, LANES), jnp.float32)
    for g in range(tiles):
        here = rows_of(second_ref, top_ref if tall else None, bottom_ref if tall else None, g)
        frame[2 * g + 1] = here
        turned = pltpu.roll(here, 64, 1)
        frame[2 * g] = jnp.where(wide, before, turned)
        before = turned
        for i, row in enumerate(win_rows):
            first[g, WIN * i : WIN * (i + 1), :] = first_ref[
                WIN * row : WIN * (row + 1), g * LANES : (g + 1) * LANES
            ]
    frame[2 * tiles] = jnp.where(wide, before, 0.0)

    def deform(step, carry):
        i, quarter = step // 4, step % 4
        row = win_rows[0] + i * (win_rows[1] - win_rows[0])
        for k in range(20):
            here = row * 80 + quarter * 20 + k
            dest = ((quarter * 4 + k // 5) * block + i * 5 + k % 5) * 8
            start = i * slab + (HALO - 1) + shift_ref[here]
            across = shift_ref[400 + here]
            tile = 2 * (quarter * 5 + k // 4) + (0, 1, 1, 2)[k % 4]
            base = (64, 32, 64, 32)[k % 4]
            lines = [frame[tile, pl.ds(start + m, 8, stride=4), :] for m in range(7)]
            ry = [taps_ref[a * 400 + here] for a in range(4)]
            rx = [taps_ref[(4 + a) * 400 + here] for a in range(4)]
            placed = []
            for j in range(4):
                mixed = (ry[0] * lines[j] + ry[1] * lines[j + 1]) + (ry[2] * lines[j + 2] + ry[3] * lines[j + 3])
                placed.append(pltpu.roll(mixed, (32 * j - base + 1 + 256 - across) & 127, 1))
            one = jnp.where(low_half, placed[0], placed[2])
            two = jnp.where(mid_half, placed[1], placed[3])
            total = rx[0] * jnp.where(even, one, two)
            for b in range(1, 4):
                total = total + rx[b] * jnp.where(even, pltpu.roll(one, LANES - b, 1), pltpu.roll(two, LANES - b, 1))
            second_win[pl.ds(pl.multiple_of(dest, 8), 8), :] = total
        for g in range(5):
            lines = [first[quarter * 5 + g, pl.ds(i * WIN + j, 8, stride=4), :] for j in range(4)]
            for w in range(4):
                k = 4 * g + w
                dest = ((quarter * 4 + k // 5) * block + i * 5 + k % 5) * 8
                turned = [pltpu.roll(lines[j], (32 * (j - w)) % LANES, 1) if j != w else lines[j] for j in range(4)]
                pair = jnp.where(even, turned[0], turned[1])
                other = jnp.where(even, turned[2], turned[3])
                first_win[pl.ds(pl.multiple_of(dest, 8), 8), :] = jnp.where(low_half, pair, other)
        return carry

    lax.fori_loop(0, 4 * count, deform, 0)

    def lift(step, carry):
        w = pl.multiple_of(step * 16, 16)
        power = []
        for side, source in enumerate((first_win, second_win)):
            at = pl.ds(pl.multiple_of(side * windows + step * 16, 16), 16)
            x = [source[pl.ds(step * 128 + l, 16, stride=8), :] for l in range(8)]
            total = ((x[0] + x[1]) + (x[2] + x[3])) + ((x[4] + x[5]) + (x[6] + x[7]))
            mean = jnp.sum(total, axis=1, keepdims=True) * (1.0 / 1024.0)
            x = [v - mean for v in x]
            q = [v * v for v in x]
            total = ((q[0] + q[1]) + (q[2] + q[3])) + ((q[4] + q[5]) + (q[6] + q[7]))
            power.append(jnp.sum(total, axis=1, keepdims=True) * (1.0 / 1024.0) + EPS)
            s = [x[l] + x[l + 4] for l in range(4)]
            d = [x[l] - x[l + 4] for l in range(4)]
            e, o = s[0] + s[2], s[1] + s[3]
            p, m = (d[1] + d[3]) * ROOT_HALF, (d[1] - d[3]) * ROOT_HALF
            for unit, value in enumerate((e + o, e - o)):
                high, low = split(value)
                pair_ends[unit, at, 0:LANES] = high
                pair_ends[unit, at, LANES : 2 * LANES] = low
            mids = ((d[0] + m, -(d[2] + p)), (s[0] - s[2], s[3] - s[1]), (d[0] - m, d[2] - p))
            for unit, parts in enumerate(mids):
                for half, value in enumerate(parts):
                    high, low = split(value)
                    pair_hi[unit, at, half * LANES : (half + 1) * LANES] = high
                    pair_lo[unit, at, half * LANES : (half + 1) * LANES] = low
        scale = (1.0 / (1024.0 * 1024.0)) / jnp.sqrt(power[0] * power[1])
        powers[pl.ds(w, 16), :] = jnp.broadcast_to(scale, (16, LANES))
        return carry

    lax.fori_loop(0, windows // 16, lift, 0)

    for unit in range(5):
        if unit < 2:
            spectrum = dot(pair_ends[unit], fwd_hi[unit]) + dot(
                pair_ends[unit, :, 0:LANES], fwd_lo[unit, 0:LANES]
            )
        else:
            spectrum = (
                dot(pair_hi[unit - 2], fwd_hi[unit])
                + dot(pair_lo[unit - 2], fwd_hi[unit])
                + dot(pair_hi[unit - 2], fwd_lo[unit])
            )
        fr, fi = spectrum[:windows, :LANES], spectrum[:windows, LANES:]
        sr, si = spectrum[windows:, :LANES], spectrum[windows:, LANES:]
        re_hi, re_lo = split(fr * sr + fi * si)
        im_hi, im_lo = split(fr * si - fi * sr)
        high = jnp.concatenate([re_hi, im_hi], axis=1)
        low = jnp.concatenate([re_lo, im_lo], axis=1)
        if unit < 2:
            table_hi, table_lo = ends_hi[unit], ends_lo[unit]
        else:
            table_hi, table_lo = mids_hi[unit - 2], mids_lo[unit - 2]
        result = dot(high, table_hi) + dot(low, table_hi) + dot(high, table_lo)
        if unit < 2:
            back[unit] = result
        else:
            back[2 * unit - 2] = result[:, :LANES]
            back[2 * unit - 1] = result[:, LANES:]

    def lower(step, carry):
        at = pl.ds(pl.multiple_of(step * 16, 16), 16)
        b0, b4, b1r, b1i, b2r, b2i, b3r, b3i = (back[u, at, :] for u in range(8))
        scale = powers[at, :]
        plus, minus = b0 + b4, b0 - b4
        evens = (plus + b2r, minus - b2i, plus - b2r, minus + b2i)
        u, v = (b1r - b3r) * ROOT_HALF, (b1i + b3i) * ROOT_HALF
        odds = (b1r + b3r, u - v, b3i - b1i, -(u + v))
        for l in range(4):
            out_ref[pl.ds(step * 128 + l, 16, stride=8), :] = 1.0 + (evens[l] + odds[l]) * scale
            out_ref[pl.ds(step * 128 + l + 4, 16, stride=8), :] = 1.0 + (evens[l] - odds[l]) * scale
        return carry

    lax.fori_loop(0, windows // 16, lower, 0)


def band_planes(win_rows, shifts, taps, first, second, halos, tables, interpret=False):
    count = len(win_rows)
    windows = BLOCKS * 5 * count
    tiles = second.shape[1] // LANES
    tall = halos is not None
    arrays = [first, second, *(halos or ()), *tables]
    vmem = pl.BlockSpec(memory_space=pltpu.VMEM)
    smem = pl.BlockSpec(memory_space=pltpu.SMEM)
    f32, bf16 = jnp.float32, jnp.bfloat16
    out = pl.pallas_call(
        functools.partial(band_kernel, win_rows, 64 if tall else 32, tall),
        out_shape=jax.ShapeDtypeStruct((windows * 8, LANES), f32),
        in_specs=[smem, smem] + [vmem] * len(arrays),
        out_specs=vmem,
        scratch_shapes=[
            pltpu.VMEM((2 * tiles + 1, 128, LANES), f32),
            pltpu.VMEM((tiles, WIN * count, LANES), f32),
            pltpu.VMEM((windows * 8, LANES), f32),
            pltpu.VMEM((windows * 8, LANES), f32),
            pltpu.VMEM((2, 2 * windows, 2 * LANES), bf16),
            pltpu.VMEM((3, 2 * windows, 2 * LANES), bf16),
            pltpu.VMEM((3, 2 * windows, 2 * LANES), bf16),
            pltpu.VMEM((windows, LANES), f32),
            pltpu.VMEM((8, windows, LANES), f32),
        ],
        compiler_params=pltpu.CompilerParams(vmem_limit_bytes=40 * 1024 * 1024),
        interpret=interpret,
        name="band_tall" if tall else "band",
    )(shifts, taps, *arrays)
    return out


def cubic_weights(fraction):
    squared = fraction * fraction
    cubed = squared * fraction
    return (
        -0.5 * cubed + squared - 0.5 * fraction,
        1.5 * cubed - 2.5 * squared + 1.0,
        -1.5 * cubed + 2.0 * squared + 0.5 * fraction,
        0.5 * cubed - 0.5 * squared,
    )


def local(first, seconds, shifts, fractions):
    second = seconds[0]
    top = lax.ppermute(second[-HALO:], "tile", [(i, i + 1) for i in range(15)])
    bottom = lax.ppermute(second[:HALO], "tile", [(i + 1, i) for i in range(15)])
    taps = jnp.stack([*cubic_weights(fractions[0]), *cubic_weights(fractions[1])]).reshape(-1)
    shifts = shifts.reshape(-1)
    tables = [jnp.asarray(t) for t in dft_tables()]
    inner = band_planes((1, 2, 3), shifts, taps, first, second, None, tables).reshape(BLOCKS, 15, 1024)
    outer = band_planes((0, 4), shifts, taps, first, second, (top, bottom), tables).reshape(BLOCKS, 10, 1024)
    both = jnp.concatenate([outer[:, :5], inner, outer[:, 5:]], axis=1)
    everything = lax.all_to_all(both, "sep", 0, 0)
    return jnp.prod(everything, axis=0).reshape(5, 5, 1024)


def solution(mesh):
    in_specs = (
        P("tile", None),
        P("sep", "tile", None),
        P(None, "sep", "tile", None),
        P(None, "sep", "tile", None),
    )
    out_specs = P("tile", "sep", None)
    return jax.shard_map(local, mesh=mesh, in_specs=in_specs, out_specs=out_specs, check_vma=False)
```

time: 405 us -> 134 us (0.33)
  the two profiles are of different devices: /device:TPU:6 before, /device:TPU:25 now
where the time goes in v1:
time: 134 us; the launch traced here: 133 us
  blocking collectives  60.5 us (45%)
  Pallas kernels  36.3 us (27%)
  local copies, waits for them, and re-layouts  21.9 us (16%)
  starting transfers between devices  7.38 us (6%)
  other arithmetic  6.83 us (5%)
    all_to_all x1, blocking collectives, local(): everything = lax.all_to_all(both, 'sep', 0, 0)  60.5 us
    pallas_call x2, Pallas kernels, band_planes(): pl.pallas_call(functools.partial(band_kernel, win_rows, 64 if tall else 3...  36.3 us
    unnamed x42, local copies, waits for them, and re-layouts  15.5 us
    unnamed x8, other arithmetic  5.58 us
    ppermute x1, starting transfers between devices, local(): top = lax.ppermute(second[-HALO:], 'tile', [(i, i + 1) for i in range(15)])  5.02 us
  transfers between devices with their start and end apart: 2, of which 0 were waited for; matrix products, arithmetic and copies ran while one was open for 7% of the time, Pallas kernels for 16%

profile of v1, /device:TPU:25, one launch (start us, length us, event | category | flops | bytes accessed | tf_op | source)
XLA Modules:
  0.0 133.1 jit_solution(13863893331976543841)
XLA Ops:
  0.0 1.7 %slice_bitcast_fusion = (f32[16,2560]{1,0:T(8,128)}, f32[16,2560]{1,0:T(8,128)}) fusion(f32[1,160,2560]{2,1,0:T(8,128)} %param.11), kind=kLoop, calls=%fused_computation.1 | loop fusion | bytes 655360 | tf_op jit(solution)/shard_map/slice | solution.py:253
  1.7 2.4 %collective-permute-start.1 = (f32[16,2560]{1,0:T(8,128)}, f32[16,2560]{1,0:T(8,128)}, u32[]{:S(2)}, u32[]{:S(2)}) collective-permute-start(f32[16,2560]{1,0:T(8,128)} %get-tuple-element.5), channel_id=1, source_target_pairs={{1,0},{2,1},{3,2},{4,3},{5,4},{6,5},{7,6},{8,7},{9,8},{10,9},{11,1... | collective-permute-start | bytes 491528 | tf_op jit(solution)/shard_map/ppermute | solution.py:253
  4.1 5.0 %collective-permute-start = (f32[16,2560]{1,0:T(8,128)}, f32[16,2560]{1,0:T(8,128)}, u32[]{:S(2)}, u32[]{:S(2)}) collective-permute-start(f32[16,2560]{1,0:T(8,128)} %get-tuple-element.6), channel_id=1, source_target_pairs={{0,1},{1,2},{2,3},{3,4},{4,5},{5,6},{6,7},{7,8},{8,9},{9,10},{10,1... | collective-permute-start | bytes 491528 | tf_op jit(solution)/shard_map/ppermute | solution.py:252
  9.1 0.7 reduce
  9.8 0.1 reshape.77.shift_ref
  9.9 0.0 copy-start.18
  9.9 0.7 constant_dynamic-update-slice_fusion.7
  10.6 0.7 constant_dynamic-update-slice_fusion.6
  11.3 0.7 constant_dynamic-update-slice_fusion.5
  12.0 0.7 constant_dynamic-update-slice_fusion.4
  12.7 0.7 constant_dynamic-update-slice_fusion.3
  13.4 0.7 constant_dynamic-update-slice_fusion.2
  14.1 0.7 constant_dynamic-update-slice_fusion.1
  14.8 0.7 constant_dynamic-update-slice_fusion
  15.5 0.1 reduce.1
  15.6 0.1 reshape.78.taps_ref
  15.6 0.0 copy-done.18
  15.6 0.0 copy-start
  15.6 1.4 %copy-done = f32[1,160,2560]{2,1,0:T(8,128)S(1)} copy-done((f32[1,160,2560]{2,1,0:T(8,128)S(1)}, f32[1,160,2560]{2,1,0:T(8,128)}, u32[]{:S(2)}) %copy-start) | copy-done | bytes 1638424
  17.1 0.0 copy-start.2
  17.1 1.4 %copy-done.2 = f32[160,2560]{1,0:T(8,128)S(1)} copy-done((f32[160,2560]{1,0:T(8,128)S(1)}, f32[160,2560]{1,0:T(8,128)}, u32[]{:S(2)}) %copy-start.2) | copy-done | bytes 1638424
  18.5 0.0 copy-start.6
  18.5 1.1 copy-done.6
  19.6 0.0 copy-start.8
  19.6 1.1 copy-done.8
  20.7 0.0 copy-start.10
  20.7 1.0 copy-done.10
  21.7 0.0 copy-start.12
  21.7 1.0 copy-done.12
  22.7 0.0 copy-start.14
  22.7 0.9 copy-done.14
  23.6 0.0 copy-start.16
  23.6 0.9 copy-done.16
  24.5 0.0 copy-start.3
  24.5 20.9 %band.1 = f32[1920,128]{1,0:T(8,128)S(1)} custom-call(s32[800]{0:T(1024)S(1)} %reshape.77.shift_ref, f32[3200]{0:T(1024)S(1)} %reshape.78.taps_ref, f32[160,2560]{1,0:T(8,128)S(1)} %copy-done.2, f32[160,2560]{1,0:T(8,128)S(1)} %bitcast.5, bf16[5,256,256]{2,1,0:T(8,128)(2,1)S(1)} %copy-done.8, bf16[5,256,256]{2,1,0:T(8,128)(2,1)S(1)} %copy-done.6, ...), custom_call_target="tpu_custom_call" | custom-call | tf_op jit(solution)/shard_map/band/pallas_call | solution.py:216
  45.4 0.0 copy-start.4
  45.4 1.0 copy-done.4
  46.4 0.0 copy-start.1
  46.4 0.0 copy-start.15
  46.4 0.0 copy-start.17
  46.4 2.4 %reshape.80 = f32[16,15,1024]{2,1,0:T(8,128)} reshape(f32[1920,128]{1,0:T(8,128)} %copy-done.4) | data formatting | bytes 1966080 | tf_op jit(solution)/shard_map/reshape | solution.py:257
  48.9 0.0 collective-permute-done.1.refs_1_
  48.9 0.0 collective-permute-done.refs_0_
  48.9 0.0 copy-done.3
  48.9 0.0 copy-done.1
  48.9 0.0 copy-done.15
  48.9 0.0 copy-done.17
  48.9 0.0 copy-start.7
  48.9 1.1 copy-done.7
  50.0 0.0 copy-start.9
  50.0 1.1 copy-done.9
  51.1 1.0 copy-done.11
  52.1 1.0 copy-done.13
  53.1 0.7 copy-done.19
  53.7 15.4 %band_tall.1 = f32[1280,128]{1,0:T(8,128)S(1)} custom-call(s32[800]{0:T(1024)S(1)} %copy-done.19, f32[3200]{0:T(1024)S(1)} %reshape.78.taps_ref, f32[160,2560]{1,0:T(8,128)S(1)} %copy-done.3, f32[160,2560]{1,0:T(8,128)S(1)} %bitcast.6, f32[16,2560]{1,0:T(8,128)} %collective-permute-done.refs_0_, f32[16,2560]{1,0:T(8,128)} %collective-permute-done.1.refs_1_, ...), custom_call_target="tpu_custom_call" | custom-call | tf_op jit(solution)/shard_map/band_tall/pallas_call | solution.py:216
  69.1 0.0 copy-start.5
  69.1 0.9 copy-done.5
  70.0 1.3 reshape.79
  71.3 0.1 fusion
  71.4 0.0 copy-done.20
  71.4 0.4 pad_maximum_fusion
  71.8 60.5 %all_to_all.5 = f32[16,25,1024]{2,1,0:T(8,128)S(1)} all-to-all(f32[16,25,1024]{2,1,0:T(8,128)S(1)} %pad_maximum_fusion), channel_id=1, replica_groups=mesh['sep'=16,'tile'=16] {'sep'}, dimensions={0} | all-to-all | bytes 3276800 | tf_op jit(solution)/shard_map/all_to_all | solution.py:260
  132.3 0.1 reduce_prod.9
  132.4 0.7 reshape.81
  (4 shorter events, 0.0 us)
Async XLA Ops:
  1.7 47.1 %collective-permute-start.1 = (f32[16,2560]{1,0:T(8,128)}, f32[16,2560]{1,0:T(8,128)}, u32[]{:S(2)}, u32[]{:S(2)}) collective-permute-start(f32[16,2560]{1,0:T(8,128)} %get-tuple-element.5), channel_id=1, source_target_pairs={{1,0},{2,1},{3,2},{4,3},{5,4},{6,5},{7,6},{8,7},{9,8},{10,9},{11,1... | collective-permute-start | bytes 491528 | tf_op jit(solution)/shard_map/ppermute | solution.py:253
  4.1 44.8 %collective-permute-start = (f32[16,2560]{1,0:T(8,128)}, f32[16,2560]{1,0:T(8,128)}, u32[]{:S(2)}, u32[]{:S(2)}) collective-permute-start(f32[16,2560]{1,0:T(8,128)} %get-tuple-element.6), channel_id=1, source_target_pairs={{0,1},{1,2},{2,3},{3,4},{4,5},{5,6},{6,7},{7,8},{8,9},{9,10},{10,1... | collective-permute-start | bytes 491528 | tf_op jit(solution)/shard_map/ppermute | solution.py:252
  9.9 5.7 %copy-start.18 = (s32[800]{0:T(1024)}, s32[800]{0:T(1024)S(1)}, u32[]{:S(2)}) copy-start(s32[800]{0:T(1024)S(1)} %reshape.77.shift_ref) | copy-start | bytes 9604
  15.6 1.4 %copy-start = (f32[1,160,2560]{2,1,0:T(8,128)S(1)}, f32[1,160,2560]{2,1,0:T(8,128)}, u32[]{:S(2)}) copy-start(f32[1,160,2560]{2,1,0:T(8,128)} %param.11) | copy-start | bytes 4915204
  17.1 1.4 %copy-start.2 = (f32[160,2560]{1,0:T(8,128)S(1)}, f32[160,2560]{1,0:T(8,128)}, u32[]{:S(2)}) copy-start(f32[160,2560]{1,0:T(8,128)} %first_ref.3) | copy-start | bytes 4915204
  18.5 1.1 copy-start.6
  19.6 1.1 copy-start.8
  20.7 1.0 copy-start.10
  21.7 1.0 copy-start.12
  22.7 0.9 copy-start.14
  23.6 0.9 copy-start.16
  24.5 24.4 %copy-start.3 = (f32[160,2560]{1,0:T(8,128)S(1)}, f32[160,2560]{1,0:T(8,128)}, u32[]{:S(2)}) copy-start(f32[160,2560]{1,0:T(8,128)} %first_ref.3) | copy-start | bytes 4915204
  45.4 1.0 copy-start.4
  46.4 2.5 %copy-start.1 = (f32[1,160,2560]{2,1,0:T(8,128)S(1)}, f32[1,160,2560]{2,1,0:T(8,128)}, u32[]{:S(2)}) copy-start(f32[1,160,2560]{2,1,0:T(8,128)} %param.11) | copy-start | bytes 4915204
  46.4 2.5 %copy-start.15 = (bf16[2,256,128]{2,1,0:T(8,128)(2,1)S(1)}, bf16[2,256,128]{2,1,0:T(8,128)(2,1)}, u32[]{:S(2)}) copy-start(bf16[2,256,128]{2,1,0:T(8,128)(2,1)} %constant.30.clone.refs_5_.refs_3_) | copy-start | bytes 393220
  46.4 2.5 %copy-start.17 = (bf16[2,256,128]{2,1,0:T(8,128)(2,1)S(1)}, bf16[2,256,128]{2,1,0:T(8,128)(2,1)}, u32[]{:S(2)}) copy-start(bf16[2,256,128]{2,1,0:T(8,128)(2,1)} %constant.29.clone.refs_4_.refs_2_) | copy-start | bytes 393220
  48.9 1.1 copy-start.7
  50.0 1.1 copy-start.9
  51.1 1.0 copy-start.11
  52.1 1.0 copy-start.13
  53.1 0.7 copy-start.19
  69.1 0.9 copy-start.5
  70.0 1.4 %copy-start.20 = (f32[16,15,1024]{2,1,0:T(8,128)S(1)}, f32[16,15,1024]{2,1,0:T(8,128)}, u32[]{:S(2)}) copy-start(f32[16,15,1024]{2,1,0:T(8,128)} %reshape.80) | copy-start | bytes 2949124

commit v2 on v1

v2 whole, which is shorter than its diff:
```python
import functools
import math

import jax
import jax.numpy as jnp
import ml_dtypes
import numpy as np
from jax import lax
from jax.experimental import pallas as pl
from jax.experimental.pallas import tpu as pltpu
from jax.sharding import PartitionSpec as P

WIN = 32
HALO = 16
EPS = 1e-06
LANES = 128
BLOCKS = 16
ROOT_HALF = math.sqrt(0.5)


def split_table(table):
    high = table.astype(ml_dtypes.bfloat16)
    low = (table - high.astype(np.float64)).astype(ml_dtypes.bfloat16)
    return high, low


def dft_tables():
    major, minor = np.divmod(np.arange(LANES), WIN)
    forward, backward = [], []
    for unit in (0, 4, 1, 2, 3):
        phase = (np.outer(major, unit + 8 * major) + np.outer(minor, minor)) % WIN
        cos = np.cos(phase * (2.0 * np.pi / WIN))
        sin = np.sin(phase * (2.0 * np.pi / WIN))
        if unit in (0, 4):
            half = np.concatenate([cos, -sin], axis=1)
            forward.append((np.concatenate([half, half]), np.concatenate([half, 0 * half])))
            backward.append(np.concatenate([cos.T, -sin.T]))
        else:
            whole = np.block([[cos, -sin], [sin, cos]])
            forward.append((whole, whole))
            backward.append(2.0 * np.block([[cos.T, sin.T], [-sin.T, cos.T]]))
    fwd_hi = np.stack([split_table(a)[0] for a, _ in forward])
    fwd_lo = np.stack([split_table(b)[1] for _, b in forward])
    ends_hi, ends_lo = split_table(np.stack(backward[:2]))
    mids_hi, mids_lo = split_table(np.stack(backward[2:]))
    return fwd_hi, fwd_lo, ends_hi, ends_lo, mids_hi, mids_lo


def split(value):
    high = value.astype(jnp.bfloat16)
    return high, (value - high.astype(jnp.float32)).astype(jnp.bfloat16)


def dot(left, right):
    return jnp.dot(left, right, preferred_element_type=jnp.float32)


def cubic_weights(fraction):
    squared = fraction * fraction
    cubed = squared * fraction
    return (
        -0.5 * cubed + squared - 0.5 * fraction,
        1.5 * cubed - 2.5 * squared + 1.0,
        -1.5 * cubed + 2.0 * squared + 0.5 * fraction,
        0.5 * cubed - 0.5 * squared,
    )


def band_kernel(win_rows, slab, tall, shift_ref, fraction_ref, first_hbm, second_hbm, *refs):
    halos, refs = (refs[:2], refs[2:]) if tall else ((), refs)
    tables_hbm, refs = refs[:6], refs[6:]
    (keep_ref, away_ref, frame, first, shifted, second_win, first_win, pair_ends, pair_hi, pair_lo, powers,
     back, taps_vmem, taps_ref, *tables, frame_sems, first_sems, table_sems) = refs
    fwd_hi, fwd_lo, ends_hi, ends_lo, mids_hi, mids_lo = tables
    count = len(win_rows)
    block = 5 * count
    windows = BLOCKS * block
    frame_rows = frame.shape[1]
    tiles = second_hbm.shape[1] // LANES
    lane = lax.broadcasted_iota(jnp.int32, (8, LANES), 1)
    low_half = lane < 64
    mid_half = (lane >= 32) & (lane < 96)
    even = (lane % 64) < 32
    own = lax.axis_index("sep")
    own_chip, own_core = own >> 1, own & 1

    if tall:
        pieces = ((halos[0], 0, 0, 16), (second_hbm, 0, 16, 48), (second_hbm, 112, 64, 48), (halos[1], 0, 112, 16))
    else:
        pieces = ((second_hbm, 16, 0, 128),)

    def frame_copies(g):
        return [
            pltpu.make_async_copy(
                ref.at[pl.ds(source, rows), pl.ds(g * LANES, LANES)],
                frame.at[2 * g + 1, pl.ds(target, rows), :],
                frame_sems.at[n, g],
            )
            for n, (ref, source, target, rows) in enumerate(pieces)
        ]

    if tall:
        lines = tuple((WIN * row, WIN * i, WIN) for i, row in enumerate(win_rows))
    else:
        lines = ((WIN * win_rows[0], 0, WIN * count),)

    def first_copies(g):
        return [
            pltpu.make_async_copy(
                first_hbm.at[pl.ds(source, rows), pl.ds(g * LANES, LANES)],
                first.at[g, pl.ds(target, rows), :],
                first_sems.at[n, g],
            )
            for n, (source, target, rows) in enumerate(lines)
        ]

    table_copies = [
        pltpu.make_async_copy(source, target, table_sems.at[n])
        for n, (source, target) in enumerate(zip(tables_hbm, tables, strict=True))
    ]
    for copies in (frame_copies, first_copies):
        for g in range(tiles):
            for copy in copies(g):
                copy.start()
    for copy in table_copies:
        copy.start()

    for axis in range(2):
        for a, values in enumerate(cubic_weights(fraction_ref[axis, 0])):
            taps_vmem[2 * a + axis, 0:5, 0:80] = values
    taps_copy = pltpu.make_async_copy(taps_vmem, taps_ref, table_sems.at[6])
    taps_copy.start()

    wide = lax.broadcasted_iota(jnp.int32, (frame_rows, LANES), 1) < 64
    before = jnp.zeros((frame_rows, LANES), jnp.float32)
    for g in range(tiles):
        for copy in frame_copies(g):
            copy.wait()
        turned = pltpu.roll(frame[2 * g + 1], 64, 1)
        frame[2 * g] = jnp.where(wide, before, turned)
        before = turned
    frame[2 * tiles] = jnp.where(wide, before, 0.0)

    for g in range(tiles):
        for copy in first_copies(g):
            copy.wait()

    def place(chip, core, i):
        turn = chip - own_chip if core == 0 else own_chip - chip
        return ((((own_core ^ core) * 8 + ((3 * turn) & 7)) * block) + i * 5) * 8

    def gather(step, carry):
        i, quarter = step >> 2, step & 3
        base = [place(quarter * 2 + (n >> 1), n & 1, i) for n in range(4)]
        for g in range(5):
            parts = [first[quarter * 5 + g, pl.ds(i * WIN + j, 8, stride=4), :] for j in range(4)]
            for w in range(4):
                k = 4 * g + w
                turned = [pltpu.roll(parts[j], (32 * (j - w)) % LANES, 1) if j != w else parts[j] for j in range(4)]
                pair = jnp.where(even, turned[0], turned[1])
                other = jnp.where(even, turned[2], turned[3])
                dest = pl.multiple_of(base[k // 5] + (k % 5) * 8, 8)
                first_win[pl.ds(dest, 8), :] = jnp.where(low_half, pair, other)
        return carry

    lax.fori_loop(0, 4 * count, gather, 0)

    taps_copy.wait()

    def mix_rows(step, k):
        i, chip = step >> 3, step & 7
        row, column = win_rows[0] + i * (win_rows[1] - win_rows[0]), chip * 10 + k
        start = i * slab + (HALO - 1) + shift_ref[0, 0, row, column]
        across = shift_ref[1, 0, row, column]
        tile = chip * 5 + (k + 1) // 2
        rows = [frame[tile, pl.ds(start + m, 8, stride=4), :] for m in range(7)]
        ry = [taps_ref[2 * a, row, column] for a in range(4)]
        turned = []
        for j in range(4):
            mixed = (ry[0] * rows[j] + ry[1] * rows[j + 1]) + (ry[2] * rows[j + 2] + ry[3] * rows[j + 3])
            turned.append(pltpu.roll(mixed, (32 * j - (64, 32)[k % 2] + 1 + 256 - across) & 127, 1))
        shifted[k, 0] = jnp.where(low_half, turned[0], turned[2])
        shifted[k, 1] = jnp.where(mid_half, turned[1], turned[3])

    def mix_columns(step, k, base):
        i, chip = step >> 3, step & 7
        row, column = win_rows[0] + i * (win_rows[1] - win_rows[0]), chip * 10 + k
        rx = [taps_ref[2 * a + 1, row, column] for a in range(4)]
        one, two = shifted[k, 0], shifted[k, 1]
        total = rx[0] * jnp.where(even, one, two)
        for b in range(1, 4):
            total = total + rx[b] * jnp.where(even, pltpu.roll(one, LANES - b, 1), pltpu.roll(two, LANES - b, 1))
        second_win[pl.ds(pl.multiple_of(base[k // 5] + (k % 5) * 8, 8), 8), :] = total

    steps = 8 * count
    for k in range(10):
        mix_rows(0, k)

    def deform(step, carry):
        base = [place(step & 7, core, step >> 3) for core in range(2)]
        later = jnp.minimum(step + 1, steps - 1)
        for k in range(10):
            mix_columns(step, k, base)
            mix_rows(later, k)
        return carry

    lax.fori_loop(0, steps, deform, 0)

    def lift(step, carry):
        w = pl.multiple_of(step * 16, 16)
        power = []
        for side, source in enumerate((first_win, second_win)):
            at = pl.ds(pl.multiple_of(side * windows + step * 16, 16), 16)
            x = [source[pl.ds(step * 128 + l, 16, stride=8), :] for l in range(8)]
            total = ((x[0] + x[1]) + (x[2] + x[3])) + ((x[4] + x[5]) + (x[6] + x[7]))
            mean = jnp.sum(total, axis=1, keepdims=True) * (1.0 / 1024.0)
            x = [v - mean for v in x]
            q = [v * v for v in x]
            total = ((q[0] + q[1]) + (q[2] + q[3])) + ((q[4] + q[5]) + (q[6] + q[7]))
            power.append(jnp.sum(total, axis=1, keepdims=True) * (1.0 / 1024.0) + EPS)
            s = [x[l] + x[l + 4] for l in range(4)]
            d = [x[l] - x[l + 4] for l in range(4)]
            e, o = s[0] + s[2], s[1] + s[3]
            p, m = (d[1] + d[3]) * ROOT_HALF, (d[1] - d[3]) * ROOT_HALF
            for unit, value in enumerate((e + o, e - o)):
                high, low = split(value)
                pair_ends[unit, at, 0:LANES] = high
                pair_ends[unit, at, LANES : 2 * LANES] = low
            mids = ((d[0] + m, -(d[2] + p)), (s[0] - s[2], s[3] - s[1]), (d[0] - m, d[2] - p))
            for unit, parts in enumerate(mids):
                for half, value in enumerate(parts):
                    high, low = split(value)
                    pair_hi[unit, at, half * LANES : (half + 1) * LANES] = high
                    pair_lo[unit, at, half * LANES : (half + 1) * LANES] = low
        scale = (1.0 / (1024.0 * 1024.0)) / jnp.sqrt(power[0] * power[1])
        powers[pl.ds(w, 16), :] = jnp.broadcast_to(scale, (16, LANES))
        return carry

    lax.fori_loop(0, windows // 16, lift, 0, unroll=5)
    for copy in table_copies:
        copy.wait()

    for unit in range(5):
        if unit < 2:
            spectrum = dot(pair_ends[unit], fwd_hi[unit]) + dot(
                pair_ends[unit, :, 0:LANES], fwd_lo[unit, 0:LANES]
            )
        else:
            spectrum = (
                dot(pair_hi[unit - 2], fwd_hi[unit])
                + dot(pair_lo[unit - 2], fwd_hi[unit])
                + dot(pair_hi[unit - 2], fwd_lo[unit])
            )
        fr, fi = spectrum[:windows, :LANES], spectrum[:windows, LANES:]
        sr, si = spectrum[windows:, :LANES], spectrum[windows:, LANES:]
        re_hi, re_lo = split(fr * sr + fi * si)
        im_hi, im_lo = split(fr * si - fi * sr)
        high = jnp.concatenate([re_hi, im_hi], axis=1)
        low = jnp.concatenate([re_lo, im_lo], axis=1)
        if unit < 2:
            table_hi, table_lo = ends_hi[unit], ends_lo[unit]
        else:
            table_hi, table_lo = mids_hi[unit - 2], mids_lo[unit - 2]
        result = dot(high, table_hi) + dot(low, table_hi) + dot(high, table_lo)
        if unit < 2:
            back[unit] = result
        else:
            back[2 * unit - 2] = result[:, :LANES]
            back[2 * unit - 1] = result[:, LANES:]

    for part, out_ref in enumerate((away_ref, keep_ref)):

        def lower(step, carry, out_ref=out_ref, offset=(1 - part) * (windows // 2)):
            at = pl.ds(pl.multiple_of(offset + step * 8, 8), 8)
            b0, b4, b1r, b1i, b2r, b2i, b3r, b3i = (back[u, at, :] for u in range(8))
            scale = powers[at, :]
            plus, minus = b0 + b4, b0 - b4
            evens = (plus + b2r, minus - b2i, plus - b2r, minus + b2i)
            u, v = (b1r - b3r) * ROOT_HALF, (b1i + b3i) * ROOT_HALF
            odds = (b1r + b3r, u - v, b3i - b1i, -(u + v))
            for l in range(4):
                out_ref[pl.ds(step * 64 + l, 8, stride=8), :] = 1.0 + (evens[l] + odds[l]) * scale
                out_ref[pl.ds(step * 64 + l + 4, 8, stride=8), :] = 1.0 + (evens[l] - odds[l]) * scale
            return carry

        lax.fori_loop(0, windows // 16, lower, 0, unroll=5)


def band_planes(win_rows, shifts, fractions, first, second, halos, tables, interpret=False):
    count = len(win_rows)
    windows = BLOCKS * 5 * count
    tiles = second.shape[1] // LANES
    tall = halos is not None
    arrays = [first, second, *(halos or ()), *tables]
    vmem = pl.BlockSpec(memory_space=pltpu.VMEM)
    smem = pl.BlockSpec(memory_space=pltpu.SMEM)
    hbm = pl.BlockSpec(memory_space=pltpu.HBM)
    f32, bf16 = jnp.float32, jnp.bfloat16
    half = jax.ShapeDtypeStruct((windows * 4, LANES), f32)
    return pl.pallas_call(
        functools.partial(band_kernel, win_rows, 64 if tall else 32, tall),
        out_shape=[half, half],
        in_specs=[smem, vmem] + [hbm] * len(arrays),
        out_specs=[vmem, vmem],
        scratch_shapes=[
            pltpu.VMEM((2 * tiles + 1, 128, LANES), f32),
            pltpu.VMEM((tiles, WIN * count, LANES), f32),
            pltpu.VMEM((10, 2, 8, LANES), f32),
            pltpu.VMEM((windows * 8, LANES), f32),
            pltpu.VMEM((windows * 8, LANES), f32),
            pltpu.VMEM((2, 2 * windows, 2 * LANES), bf16),
            pltpu.VMEM((3, 2 * windows, 2 * LANES), bf16),
            pltpu.VMEM((3, 2 * windows, 2 * LANES), bf16),
            pltpu.VMEM((windows, LANES), f32),
            pltpu.VMEM((8, windows, LANES), f32),
            pltpu.VMEM((8, 8, LANES), f32),
            pltpu.SMEM((8, 8, LANES), f32),
            *(pltpu.VMEM(t.shape, t.dtype) for t in tables),
            pltpu.SemaphoreType.DMA((4, tiles)),
            pltpu.SemaphoreType.DMA((2, tiles)),
            pltpu.SemaphoreType.DMA((7,)),
        ],
        compiler_params=pltpu.CompilerParams(vmem_limit_bytes=24 * 1024 * 1024),
        interpret=interpret,
        name="band_tall" if tall else "band",
    )(shifts, fractions, *(pltpu.with_memory_space_constraint(a, pltpu.HBM) for a in arrays))


def along_z(array, hops):
    pairs = [(2 * z + c, 2 * ((z + (hops, -hops)[c]) % 8) + c) for z in range(8) for c in range(2)]
    return lax.ppermute(array, "sep", pairs)


def reduced(keep, away):
    size = keep.shape[0] // 8
    parts = keep * lax.ppermute(away, "sep", [(s, s ^ 1) for s in range(16)])
    ahead = along_z(parts[3 * size : 5 * size], 1)
    behind = along_z(parts[5 * size :], -1)
    near = parts[: 3 * size] * behind
    third = along_z(near[size : 2 * size] * ahead[size:], 3)
    sixth = along_z(near[2 * size :], -2)
    return near[:size] * ahead[:size] * third * sixth


def local(first, seconds, shifts, fractions):
    second = seconds[0]
    top = lax.ppermute(second[-HALO:], "tile", [(i, i + 1) for i in range(15)])
    bottom = lax.ppermute(second[:HALO], "tile", [(i + 1, i) for i in range(15)])
    tables = [jnp.asarray(t) for t in dft_tables()]
    inner = band_planes((1, 2, 3), shifts, fractions, first, second, None, tables)
    inner, (top, bottom) = lax.optimization_barrier((inner, (top, bottom)))
    outer = band_planes((0, 4), shifts, fractions, first, second, (top, bottom), tables)
    inner = reduced(*inner).reshape(3, 5, 1024)
    outer = reduced(*outer).reshape(2, 5, 1024)
    return jnp.concatenate([outer[:1], inner, outer[1:]], axis=0)


def solution(mesh):
    in_specs = (
        P("tile", None),
        P("sep", "tile", None),
        P(None, "sep", "tile", None),
        P(None, "sep", "tile", None),
    )
    out_specs = P("tile", "sep", None)
    return jax.shard_map(local, mesh=mesh, in_specs=in_specs, out_specs=out_specs, check_vma=False)
```

time: 134 us -> 72.6 us (0.54)
  the two profiles are of different devices: /device:TPU:25 before, /device:TPU:6 now
where the time goes in v2:
time: 72.6 us; the launch traced here: 72.4 us
  Pallas kernels  27 us (37%)
  starting transfers between devices  22.3 us (31%)
  waiting for transfers between devices  18.9 us (26%)
  local copies, waits for them, and re-layouts  3.15 us (4%)
  other arithmetic  0.88 us (1%)
    pallas_call x2, Pallas kernels, band_planes(): pl.pallas_call(functools.partial(band_kernel, win_rows, 64 if tall else 3...  27 us
    ppermute x8, waiting for transfers between devices, along_z(): return lax.ppermute(array, 'sep', pairs)  17.3 us
    ppermute x8, starting transfers between devices, along_z(): return lax.ppermute(array, 'sep', pairs)  14.2 us
    ppermute x1, starting transfers between devices, local(): lax.ppermute(second[:HALO], 'tile', [(i + 1, i) for i in range(15)])  4.47 us
    ppermute x1, starting transfers between devices, local(): top = lax.ppermute(second[-HALO:], 'tile', [(i, i + 1) for i in range(15)])  3.48 us
    unnamed x6, local copies, waits for them, and re-layouts  2.07 us
    ppermute x2, waiting for transfers between devices, reduced(): parts = keep * lax.ppermute(away, 'sep', [(s, s ^ 1) for s in range(16)])  1.62 us
  transfers between devices with their start and end apart: 12, of which 7 were waited for; matrix products, arithmetic and copies ran while one was open for 2% of the time, Pallas kernels for 21%

profile of v2, /device:TPU:6, one launch (start us, length us, event | category | flops | bytes accessed | tf_op | source)
XLA Modules:
  0.0 72.4 jit_solution(6128438054969946999)
XLA Ops:
  0.0 1.0 %slice_bitcast_fusion = (f32[16,2560]{1,0:T(8,128)S(1)}, f32[16,2560]{1,0:T(8,128)S(1)}) fusion(f32[1,160,2560]{2,1,0:T(8,128)} %param.11), kind=kLoop, calls=%fused_computation.2 | loop fusion | bytes 655360 | tf_op jit(solution)/shard_map/slice | solution.py:348
  1.0 3.5 %collective-permute-start = (f32[16,2560]{1,0:T(8,128)S(1)}, f32[16,2560]{1,0:T(8,128)S(1)}, u32[]{:S(2)}, u32[]{:S(2)}) collective-permute-start(f32[16,2560]{1,0:T(8,128)S(1)} %get-tuple-element.22), channel_id=1, source_target_pairs={{0,1},{1,2},{2,3},{3,4},{4,5},{5,6},{6,7},{7,8},{8,9},{9,10},{10,1... | collective-permute-start | bytes 491528 | tf_op jit(solution)/shard_map/ppermute | solution.py:347
  4.5 4.5 %collective-permute-start.1 = (f32[16,2560]{1,0:T(8,128)S(1)}, f32[16,2560]{1,0:T(8,128)S(1)}, u32[]{:S(2)}, u32[]{:S(2)}) collective-permute-start(f32[16,2560]{1,0:T(8,128)S(1)} %get-tuple-element.21), channel_id=1, source_target_pairs={{1,0},{2,1},{3,2},{4,3},{5,4},{6,5},{7,6},{8,7},{9,8},{10,9},{11,1... | collective-permute-start | bytes 491528 | tf_op jit(solution)/shard_map/ppermute | solution.py:348
  9.0 0.7 copy.17.shift_ref
  9.7 0.7 copy.18.fraction_ref
  10.4 15.1 %band.1 = (f32[960,128]{1,0:T(8,128)S(1)}, f32[960,128]{1,0:T(8,128)S(1)}) custom-call(s32[2,1,5,80]{3,2,1,0:T(8,128)S(1)} %copy.17.shift_ref, f32[2,1,5,80]{3,2,1,0:T(8,128)S(1)} %copy.18.fraction_ref, f32[160,2560]{1,0:T(8,128)} %first_hbm.3, f32[160,2560]{1,0:T(8,128)} %bitcast.5, bf16[5,256,256]{2,1,0:T(8,128)(2,1)} %constant.12.clone.refs_0_.refs_2_, ...), custom_call_target="tpu_custom_call" | custom-call | tf_op jit(solution)/shard_map/band/pallas_call | solution.py:300
  25.5 0.0 collective-permute-done.refs_0_
  25.5 0.0 copy-start
  25.5 0.0 collective-permute-done.1.refs_1_
  25.5 0.0 copy-start.1
  25.5 0.6 copy-done
  26.2 0.0 copy-done.1
  26.2 11.9 %band_tall.1 = (f32[640,128]{1,0:T(8,128)S(1)}, f32[640,128]{1,0:T(8,128)S(1)}) custom-call(s32[2,1,5,80]{3,2,1,0:T(8,128)S(1)} %copy.17.shift_ref, f32[2,1,5,80]{3,2,1,0:T(8,128)S(1)} %copy.18.fraction_ref, f32[160,2560]{1,0:T(8,128)} %first_hbm.3, f32[160,2560]{1,0:T(8,128)} %bitcast.6, f32[16,2560]{1,0:T(8,128)} %copy-done, f32[16,2560]{1,0:T(8,128)} %copy-done.1, ...), custom_call_target="tpu_custom_call" | custom-call | tf_op jit(solution)/shard_map/band_tall/pallas_call | solution.py:300
  38.1 0.1 collective-permute-start.2
  38.2 1.6 %collective-permute-done.2 = f32[640,128]{1,0:T(8,128)S(1)} collective-permute-done((f32[640,128]{1,0:T(8,128)S(1)}, f32[640,128]{1,0:T(8,128)S(1)}, u32[]{:S(2)}, u32[]{:S(2)}) %collective-permute-start.2) | collective-permute-done | bytes 327712 | tf_op jit(solution)/shard_map/ppermute | solution.py:336
  39.9 5.9 %collective-permute-start.3 = (f32[240,128]{1,0:T(8,128)S(1)}, f32[240,128]{1,0:T(8,128)S(1)}, u32[]{:S(2)}, u32[]{:S(2)}) collective-permute-start(f32[240,128]{1,0:T(8,128)S(1)} %slice.97), channel_id=1, source_target_pairs={{0,224},{16,48},{32,0},{48,80},{64,32},{80,112},{96,64},{112,144},... | collective-permute-start | bytes 368648 | tf_op jit(solution)/shard_map/ppermute | solution.py:331
  45.8 0.0 collective-permute-start.7
  45.8 0.1 collective-permute-start.4
  45.9 3.1 %collective-permute-done.3 = f32[240,128]{1,0:T(8,128)S(1)} collective-permute-done((f32[240,128]{1,0:T(8,128)S(1)}, f32[240,128]{1,0:T(8,128)S(1)}, u32[]{:S(2)}, u32[]{:S(2)}) %collective-permute-start.3) | collective-permute-done | bytes 122912 | tf_op jit(solution)/shard_map/ppermute | solution.py:331
  49.1 2.5 %collective-permute-done.4 = f32[160,128]{1,0:T(8,128)S(1)} collective-permute-done((f32[160,128]{1,0:T(8,128)S(1)}, f32[160,128]{1,0:T(8,128)S(1)}, u32[]{:S(2)}, u32[]{:S(2)}) %collective-permute-start.4) | collective-permute-done | bytes 81952 | tf_op jit(solution)/shard_map/ppermute | solution.py:331
  51.6 0.5 collective-permute-start.5
  52.1 1.9 %collective-permute-start.6 = (f32[80,128]{1,0:T(8,128)S(1)}, f32[80,128]{1,0:T(8,128)S(1)}, u32[]{:S(2)}, u32[]{:S(2)}) collective-permute-start(f32[80,128]{1,0:T(8,128)S(1)} %get-tuple-element.26), channel_id=1, source_target_pairs={{0,192},{16,80},{32,224},{48,112},{64,0},{80,144},{96,32},{112,176... | collective-permute-start | bytes 122888 | tf_op jit(solution)/shard_map/ppermute | solution.py:331
  54.0 0.0 collective-permute-done.7
  54.0 0.1 mul.42
  54.1 3.3 %collective-permute-start.8 = (f32[360,128]{1,0:T(8,128)S(1)}, f32[360,128]{1,0:T(8,128)S(1)}, u32[]{:S(2)}, u32[]{:S(2)}) collective-permute-start(f32[360,128]{1,0:T(8,128)S(1)} %slice.106), channel_id=1, source_target_pairs={{0,224},{16,48},{32,0},{48,80},{64,32},{80,112},{96,64},{112,144},... | collective-permute-start | bytes 552968 | tf_op jit(solution)/shard_map/ppermute | solution.py:331
  57.4 0.0 collective-permute-start.9
  57.4 2.5 %collective-permute-done.5 = f32[80,128]{1,0:T(8,128)S(1)} collective-permute-done((f32[80,128]{1,0:T(8,128)S(1)}, f32[80,128]{1,0:T(8,128)S(1)}, u32[]{:S(2)}, u32[]{:S(2)}) %collective-permute-start.5) | collective-permute-done | bytes 40992 | tf_op jit(solution)/shard_map/ppermute | solution.py:331
  59.9 0.0 collective-permute-done.6
  59.9 1.3 %collective-permute-done.8 = f32[360,128]{1,0:T(8,128)S(1)} collective-permute-done((f32[360,128]{1,0:T(8,128)S(1)}, f32[360,128]{1,0:T(8,128)S(1)}, u32[]{:S(2)}, u32[]{:S(2)}) %collective-permute-start.8) | collective-permute-done | bytes 184352 | tf_op jit(solution)/shard_map/ppermute | solution.py:331
  61.3 2.2 %collective-permute-done.9 = f32[240,128]{1,0:T(8,128)S(1)} collective-permute-done((f32[240,128]{1,0:T(8,128)S(1)}, f32[240,128]{1,0:T(8,128)S(1)}, u32[]{:S(2)}, u32[]{:S(2)}) %collective-permute-start.9) | collective-permute-done | bytes 122912 | tf_op jit(solution)/shard_map/ppermute | solution.py:331
  63.5 1.1 %collective-permute-start.10 = (f32[120,128]{1,0:T(8,128)S(1)}, f32[120,128]{1,0:T(8,128)S(1)}, u32[]{:S(2)}, u32[]{:S(2)}) collective-permute-start(f32[120,128]{1,0:T(8,128)S(1)} %get-tuple-element.23), channel_id=1, source_target_pairs={{0,96},{16,176},{32,128},{48,208},{64,160},{80,240},{96,192},{112,... | collective-permute-start | bytes 184328 | tf_op jit(solution)/shard_map/ppermute | solution.py:331
  64.6 1.4 %collective-permute-start.11 = (f32[120,128]{1,0:T(8,128)S(1)}, f32[120,128]{1,0:T(8,128)S(1)}, u32[]{:S(2)}, u32[]{:S(2)}) collective-permute-start(f32[120,128]{1,0:T(8,128)S(1)} %get-tuple-element.24), channel_id=1, source_target_pairs={{0,192},{16,80},{32,224},{48,112},{64,0},{80,144},{96,32},{112,176... | collective-permute-start | bytes 184328 | tf_op jit(solution)/shard_map/ppermute | solution.py:331
  66.0 5.6 %collective-permute-done.10 = f32[120,128]{1,0:T(8,128)S(1)} collective-permute-done((f32[120,128]{1,0:T(8,128)S(1)}, f32[120,128]{1,0:T(8,128)S(1)}, u32[]{:S(2)}, u32[]{:S(2)}) %collective-permute-start.10) | collective-permute-done | bytes 61472 | tf_op jit(solution)/shard_map/ppermute | solution.py:331
  71.7 0.0 collective-permute-done.11
  71.7 0.7 pad_maximum_fusion
  (15 shorter events, 0.2 us)
Async XLA Ops:
  1.0 24.5 %collective-permute-start = (f32[16,2560]{1,0:T(8,128)S(1)}, f32[16,2560]{1,0:T(8,128)S(1)}, u32[]{:S(2)}, u32[]{:S(2)}) collective-permute-start(f32[16,2560]{1,0:T(8,128)S(1)} %get-tuple-element.22), channel_id=1, source_target_pairs={{0,1},{1,2},{2,3},{3,4},{4,5},{5,6},{6,7},{7,8},{8,9},{9,10},{10,1... | collective-permute-start | bytes 491528 | tf_op jit(solution)/shard_map/ppermute | solution.py:347
  4.5 21.0 %collective-permute-start.1 = (f32[16,2560]{1,0:T(8,128)S(1)}, f32[16,2560]{1,0:T(8,128)S(1)}, u32[]{:S(2)}, u32[]{:S(2)}) collective-permute-start(f32[16,2560]{1,0:T(8,128)S(1)} %get-tuple-element.21), channel_id=1, source_target_pairs={{1,0},{2,1},{3,2},{4,3},{5,4},{6,5},{7,6},{8,7},{9,8},{10,9},{11,1... | collective-permute-start | bytes 491528 | tf_op jit(solution)/shard_map/ppermute | solution.py:348
  25.5 0.7 copy-start
  25.5 0.7 copy-start.1
  38.1 1.7 %collective-permute-start.2 = (f32[640,128]{1,0:T(8,128)S(1)}, f32[640,128]{1,0:T(8,128)S(1)}, u32[]{:S(2)}, u32[]{:S(2)}) collective-permute-start(f32[640,128]{1,0:T(8,128)S(1)} %get-tuple-element.18), channel_id=1, source_target_pairs={{0,16},{16,0},{32,48},{48,32},{64,80},{80,64},{96,112},{112,96},{1... | collective-permute-start | bytes 983048 | tf_op jit(solution)/shard_map/ppermute | solution.py:336
  39.9 9.1 %collective-permute-start.3 = (f32[240,128]{1,0:T(8,128)S(1)}, f32[240,128]{1,0:T(8,128)S(1)}, u32[]{:S(2)}, u32[]{:S(2)}) collective-permute-start(f32[240,128]{1,0:T(8,128)S(1)} %slice.97), channel_id=1, source_target_pairs={{0,224},{16,48},{32,0},{48,80},{64,32},{80,112},{96,64},{112,144},... | collective-permute-start | bytes 368648 | tf_op jit(solution)/shard_map/ppermute | solution.py:331
  45.8 8.2 %collective-permute-start.7 = (f32[960,128]{1,0:T(8,128)S(1)}, f32[960,128]{1,0:T(8,128)S(1)}, u32[]{:S(2)}, u32[]{:S(2)}) collective-permute-start(f32[960,128]{1,0:T(8,128)S(1)} %get-tuple-element.20), channel_id=1, source_target_pairs={{0,16},{16,0},{32,48},{48,32},{64,80},{80,64},{96,112},{112,96},{1... | collective-permute-start | bytes 1474568 | tf_op jit(solution)/shard_map/ppermute | solution.py:336
  45.8 5.7 %collective-permute-start.4 = (f32[160,128]{1,0:T(8,128)S(1)}, f32[160,128]{1,0:T(8,128)S(1)}, u32[]{:S(2)}, u32[]{:S(2)}) collective-permute-start(f32[160,128]{1,0:T(8,128)S(1)} %slice.99), channel_id=1, source_target_pairs={{0,32},{16,240},{32,64},{48,16},{64,96},{80,48},{96,128},{112,80},... | collective-permute-start | bytes 245768 | tf_op jit(solution)/shard_map/ppermute | solution.py:331
  51.6 8.3 %collective-permute-start.5 = (f32[80,128]{1,0:T(8,128)S(1)}, f32[80,128]{1,0:T(8,128)S(1)}, u32[]{:S(2)}, u32[]{:S(2)}) collective-permute-start(f32[80,128]{1,0:T(8,128)S(1)} %get-tuple-element.25), channel_id=1, source_target_pairs={{0,96},{16,176},{32,128},{48,208},{64,160},{80,240},{96,192},{112,... | collective-permute-start | bytes 122888 | tf_op jit(solution)/shard_map/ppermute | solution.py:331
  52.1 7.8 %collective-permute-start.6 = (f32[80,128]{1,0:T(8,128)S(1)}, f32[80,128]{1,0:T(8,128)S(1)}, u32[]{:S(2)}, u32[]{:S(2)}) collective-permute-start(f32[80,128]{1,0:T(8,128)S(1)} %get-tuple-element.26), channel_id=1, source_target_pairs={{0,192},{16,80},{32,224},{48,112},{64,0},{80,144},{96,32},{112,176... | collective-permute-start | bytes 122888 | tf_op jit(solution)/shard_map/ppermute | solution.py:331
  54.1 7.2 %collective-permute-start.8 = (f32[360,128]{1,0:T(8,128)S(1)}, f32[360,128]{1,0:T(8,128)S(1)}, u32[]{:S(2)}, u32[]{:S(2)}) collective-permute-start(f32[360,128]{1,0:T(8,128)S(1)} %slice.106), channel_id=1, source_target_pairs={{0,224},{16,48},{32,0},{48,80},{64,32},{80,112},{96,64},{112,144},... | collective-permute-start | bytes 552968 | tf_op jit(solution)/shard_map/ppermute | solution.py:331
  57.4 6.1 %collective-permute-start.9 = (f32[240,128]{1,0:T(8,128)S(1)}, f32[240,128]{1,0:T(8,128)S(1)}, u32[]{:S(2)}, u32[]{:S(2)}) collective-permute-start(f32[240,128]{1,0:T(8,128)S(1)} %slice.108), channel_id=1, source_target_pairs={{0,32},{16,240},{32,64},{48,16},{64,96},{80,48},{96,128},{112,80},... | collective-permute-start | bytes 368648 | tf_op jit(solution)/shard_map/ppermute | solution.py:331
  63.5 8.1 %collective-permute-start.10 = (f32[120,128]{1,0:T(8,128)S(1)}, f32[120,128]{1,0:T(8,128)S(1)}, u32[]{:S(2)}, u32[]{:S(2)}) collective-permute-start(f32[120,128]{1,0:T(8,128)S(1)} %get-tuple-element.23), channel_id=1, source_target_pairs={{0,96},{16,176},{32,128},{48,208},{64,160},{80,240},{96,192},{112,... | collective-permute-start | bytes 184328 | tf_op jit(solution)/shard_map/ppermute | solution.py:331
  64.6 7.0 %collective-permute-start.11 = (f32[120,128]{1,0:T(8,128)S(1)}, f32[120,128]{1,0:T(8,128)S(1)}, u32[]{:S(2)}, u32[]{:S(2)}) collective-permute-start(f32[120,128]{1,0:T(8,128)S(1)} %get-tuple-element.24), channel_id=1, source_target_pairs={{0,192},{16,80},{32,224},{48,112},{64,0},{80,144},{96,32},{112,176... | collective-permute-start | bytes 184328 | tf_op jit(solution)/shard_map/ppermute | solution.py:331

commit v3 on v2

v3 whole, which is shorter than its diff:
```python
import functools
import math

import jax
import jax.numpy as jnp
import ml_dtypes
import numpy as np
from jax import lax
from jax.experimental import pallas as pl
from jax.experimental.pallas import tpu as pltpu
from jax.sharding import PartitionSpec as P

WIN = 32
HALO = 16
EPS = 1e-06
LANES = 128
BLOCKS = 16
ROOT_HALF = math.sqrt(0.5)


def split_table(table):
    high = table.astype(ml_dtypes.bfloat16)
    low = (table - high.astype(np.float64)).astype(ml_dtypes.bfloat16)
    return high, low


def dft_tables():
    major, minor = np.divmod(np.arange(LANES), WIN)
    high, low = [], []
    for unit in (0, 4, 1, 2, 3):
        phase = (np.outer(major, unit + 8 * major) + np.outer(minor, minor)) % WIN
        cos = np.cos(phase * (2.0 * np.pi / WIN))
        sin = np.sin(phase * (2.0 * np.pi / WIN))
        if unit in (0, 4):
            table = np.concatenate([np.concatenate([cos, -sin], axis=1)] * 2)
        else:
            table = np.block([[cos, -sin], [sin, cos]])
        high.append(split_table(table)[0])
        low.append(split_table(table)[1])
    return np.stack(high), np.stack(low)


def split(value):
    high = value.astype(jnp.bfloat16)
    return high, (value - high.astype(jnp.float32)).astype(jnp.bfloat16)


def dot(left, right):
    return jnp.dot(left, right, preferred_element_type=jnp.float32)


def dot_back(left, right):
    return lax.dot_general(left, right, (((1,), (1,)), ((), ())), preferred_element_type=jnp.float32)


def cubic_weights(fraction):
    squared = fraction * fraction
    cubed = squared * fraction
    return (
        -0.5 * cubed + squared - 0.5 * fraction,
        1.5 * cubed - 2.5 * squared + 1.0,
        -1.5 * cubed + 2.0 * squared + 0.5 * fraction,
        0.5 * cubed - 0.5 * squared,
    )


def masks():
    lane = lax.broadcasted_iota(jnp.int32, (8, LANES), 1)
    return lane, lane < 64, (lane % 64) < 32


def place(chip, core, i, block):
    own = lax.axis_index("sep")
    own_chip, own_core = own >> 1, own & 1
    turn = chip - own_chip if core == 0 else own_chip - chip
    return ((((own_core ^ core) * 8 + ((3 * turn) & 7)) * block) + i * 5) * 8


def lift_windows(source, pair_ends, pair_hi, pair_lo, finish):
    def lift(step, carry):
        at = pl.ds(pl.multiple_of(step * 16, 16), 16)
        x = [source[pl.ds(step * 128 + l, 16, stride=8), :] for l in range(8)]
        total = ((x[0] + x[1]) + (x[2] + x[3])) + ((x[4] + x[5]) + (x[6] + x[7]))
        mean = jnp.sum(total, axis=1, keepdims=True) * (1.0 / 1024.0)
        x = [v - mean for v in x]
        q = [v * v for v in x]
        total = ((q[0] + q[1]) + (q[2] + q[3])) + ((q[4] + q[5]) + (q[6] + q[7]))
        finish(at, jnp.sum(total, axis=1, keepdims=True) * (1.0 / 1024.0) + EPS)
        s = [x[l] + x[l + 4] for l in range(4)]
        d = [x[l] - x[l + 4] for l in range(4)]
        e, o = s[0] + s[2], s[1] + s[3]
        p, m = (d[1] + d[3]) * ROOT_HALF, (d[1] - d[3]) * ROOT_HALF
        for unit, value in enumerate((e + o, e - o)):
            high, low = split(value)
            pair_ends[unit, at, 0:LANES] = high
            pair_ends[unit, at, LANES : 2 * LANES] = low
        mids = ((d[0] + m, -(d[2] + p)), (s[0] - s[2], s[3] - s[1]), (d[0] - m, d[2] - p))
        for unit, parts in enumerate(mids):
            for half, value in enumerate(parts):
                high, low = split(value)
                pair_hi[unit, at, half * LANES : (half + 1) * LANES] = high
                pair_lo[unit, at, half * LANES : (half + 1) * LANES] = low
        return carry

    lax.fori_loop(0, source.shape[0] // 128, lift, 0, unroll=5)


def spectrum_of(unit, pair_ends, pair_hi, pair_lo, table_hi, table_lo):
    hi, lo = table_hi[unit], table_lo[unit]
    if unit < 2:
        return dot(pair_ends[unit], hi) + dot(pair_ends[unit, :, 0:LANES], lo[0:LANES])
    return dot(pair_hi[unit - 2], hi) + dot(pair_lo[unit - 2], hi) + dot(pair_hi[unit - 2], lo)


def first_kernel(first_hbm, high_hbm, low_hbm, spectra_ref, power_ref,
                 first, first_win, pair_ends, pair_hi, pair_lo, table_hi, table_lo, first_sems, table_sems):
    win_rows = first_hbm.shape[0] // WIN
    block = first_win.shape[0] // 8 // BLOCKS
    lane, low_half, even = masks()
    outer_blocks = (lane < 32) | (lane >= 96)
    first_copies = [
        pltpu.make_async_copy(first_hbm.at[:, pl.ds(g * LANES, LANES)], first.at[g], first_sems.at[g])
        for g in range(first.shape[0])
    ]
    table_copies = [
        pltpu.make_async_copy(high_hbm, table_hi, table_sems.at[0]),
        pltpu.make_async_copy(low_hbm, table_lo, table_sems.at[1]),
    ]
    for copy in first_copies + table_copies:
        copy.start()
    for copy in first_copies:
        copy.wait()

    def gather(step, carry):
        i, quarter = step >> 2, step & 3
        base = [place(quarter * 2 + (n >> 1), n & 1, i, block) for n in range(4)]
        for g in range(5):
            v = [first[quarter * 5 + g, pl.ds(i * WIN + j, 8, stride=4), :] for j in range(4)]
            turned = pltpu.roll(jnp.where(outer_blocks, v[2], v[0]), 64, 1)
            p = jnp.where(low_half, jnp.where(even, v[0], v[2]), turned)
            q = jnp.where(low_half, turned, jnp.where(even, v[2], v[0]))
            turned = pltpu.roll(jnp.where(low_half, v[3], v[1]), 64, 1)
            r = jnp.where(low_half, v[1], turned)
            s = jnp.where(low_half, turned, v[3])
            for w, (one, two) in ((0, (p, r)), (2, (q, s))):
                turned = pltpu.roll(jnp.where(even, two, one), 32, 1)
                for k, value in (
                    (4 * g + w, jnp.where(even, one, turned)),
                    (4 * g + w + 1, jnp.where(even, turned, two)),
                ):
                    first_win[pl.ds(pl.multiple_of(base[k // 5] + (k % 5) * 8, 8), 8), :] = value
        return carry

    lax.fori_loop(0, 4 * win_rows, gather, 0, unroll=2)


    def finish(at, power):
        power_ref[at, :] = jnp.broadcast_to(power, (16, LANES))

    lift_windows(first_win, pair_ends, pair_hi, pair_lo, finish)
    for copy in table_copies:
        copy.wait()
    for unit in range(5):
        spectra_ref[unit] = spectrum_of(unit, pair_ends, pair_hi, pair_lo, table_hi, table_lo)


def band_kernel(shift_hbm, fraction_hbm, second_hbm, top_hbm, bottom_hbm, high_hbm, low_hbm, spectra_ref, power_ref,
                keep_ref, away_ref, frame, swapped, shifted, second_win,
                pair_ends, pair_hi, pair_lo, powers, back, fraction_ref, shift_ref, taps_vmem, taps_ref,
                table_hi, table_lo, frame_sems, small_sems):
    windows = second_win.shape[0] // 8
    band = second_hbm.shape[0]
    win_rows = band // WIN
    block = windows // BLOCKS
    tiles = second_hbm.shape[1] // LANES
    lane, low_half, even = masks()

    small_copies = [
        pltpu.make_async_copy(fraction_hbm, fraction_ref, small_sems.at[0]),
        pltpu.make_async_copy(shift_hbm, shift_ref, small_sems.at[1]),
    ]
    table_copies = [
        pltpu.make_async_copy(high_hbm, table_hi, small_sems.at[2]),
        pltpu.make_async_copy(low_hbm, table_lo, small_sems.at[3]),
    ]
    frame_copies = [
        pltpu.make_async_copy(
            ref.at[:, pl.ds(g * LANES, LANES)],
            frame.at[2 * g + 1, pl.ds(row, rows), :],
            frame_sems.at[n, g],
        )
        for n, (ref, row, rows) in enumerate(
            ((second_hbm, HALO, band), (top_hbm, 0, HALO), (bottom_hbm, HALO + band, HALO))
        )
        for g in range(tiles)
    ]
    for copy in small_copies + frame_copies + table_copies:
        copy.start()

    for copy in small_copies:
        copy.wait()
    for axis in range(2):
        for a, values in enumerate(cubic_weights(fraction_ref[axis, :, 0, :])):
            taps_vmem[2 * a + axis, 0:5, 0:80] = values
    taps_copy = pltpu.make_async_copy(taps_vmem, taps_ref, small_sems.at[4])
    taps_copy.start()

    for copy in frame_copies:
        copy.wait()
    wide = lax.broadcasted_iota(jnp.int32, (16, LANES), 1) < 64

    def fill(step, carry):
        rows = pl.ds(pl.multiple_of(step * 16, 16), 16)
        before = before_turned = jnp.zeros((16, LANES), jnp.float32)
        for g in range(tiles):
            here = frame[2 * g + 1, rows, :]
            turned = pltpu.roll(here, 64, 1)
            swapped[2 * g + 1, rows, :] = turned
            frame[2 * g, rows, :] = jnp.where(wide, before_turned, turned)
            swapped[2 * g, rows, :] = jnp.where(wide, here, before)
            before, before_turned = here, turned
        frame[2 * tiles, rows, :] = jnp.where(wide, before_turned, 0.0)
        swapped[2 * tiles, rows, :] = jnp.where(wide, 0.0, before)
        return carry

    lax.fori_loop(0, frame.shape[1] // 16, fill, 0)
    taps_copy.wait()

    def mix_rows(step, k):
        i, column = step >> 3, (step & 7) * 10 + k
        start = i * WIN + (HALO - 1) + shift_ref[0, i, 0, column]
        tile = (step & 7) * 5 + (k + 1) // 2
        base = (64, 32)[k % 2]
        turn = 257 - base - shift_ref[1, i, 0, column]
        ry = [taps_ref[2 * a, i, column] for a in range(4)]
        inside = (lane >= base - 16) & (lane < base + 48)
        rows = [frame[tile, pl.ds(start + m, 8, stride=4), :] for m in range(5)]
        others = [swapped[tile, pl.ds(start + 2 + m, 8, stride=4), :] for m in range(5)]
        mixed = []
        for j in range(2):
            one = (ry[0] * rows[j] + ry[1] * rows[j + 1]) + (ry[2] * rows[j + 2] + ry[3] * rows[j + 3])
            two = (ry[0] * others[j] + ry[1] * others[j + 1]) + (ry[2] * others[j + 2] + ry[3] * others[j + 3])
            mixed.append(pltpu.roll(jnp.where(inside, one, two), (turn + 32 * j) & 127, 1))
        shifted[k, 0] = jnp.where(even, mixed[0], mixed[1])
        shifted[k, 1] = jnp.where(even, mixed[1], mixed[0])

    def mix_columns(step, k, base):
        i, column = step >> 3, (step & 7) * 10 + k
        rx = [taps_ref[2 * a + 1, i, column] for a in range(4)]
        one, following = shifted[k, 0], shifted[k, 1]
        total = rx[0] * one
        for b in range(1, 4):
            total = total + rx[b] * pltpu.roll(jnp.where((lane & 31) < b, following, one), LANES - b, 1)
        second_win[pl.ds(pl.multiple_of(base[k // 5] + (k % 5) * 8, 8), 8), :] = total

    steps = 8 * win_rows
    for k in range(10):
        mix_rows(0, k)

    def deform(step, carry):
        base = [place(step & 7, core, step >> 3, block) for core in range(2)]
        later = jnp.minimum(step + 1, steps - 1)
        for k in range(10):
            mix_columns(step, k, base)
            mix_rows(later, k)
        return carry

    lax.fori_loop(0, steps, deform, 0)

    def finish(at, power):
        scale = (2.0 / (1024.0 * 1024.0)) / jnp.sqrt(power_ref[at, :] * power)
        powers[at, :] = scale

    lift_windows(second_win, pair_ends, pair_hi, pair_lo, finish)
    for copy in table_copies:
        copy.wait()

    for unit in range(5):
        second = spectrum_of(unit, pair_ends, pair_hi, pair_lo, table_hi, table_lo)
        fr, fi = spectra_ref[unit, :, :LANES], spectra_ref[unit, :, LANES:]
        sr, si = second[:, :LANES], second[:, LANES:]
        re_hi, re_lo = split(fr * sr + fi * si)
        im_hi, im_lo = split(fr * si - fi * sr)
        high = jnp.concatenate([re_hi, im_hi], axis=1)
        low = jnp.concatenate([re_lo, im_lo], axis=1)
        rows = LANES if unit < 2 else 2 * LANES
        hi, lo = table_hi[unit, 0:rows], table_lo[unit, 0:rows]
        result = dot_back(high, hi) + dot_back(low, hi) + dot_back(high, lo)
        if unit < 2:
            back[unit] = result
        else:
            back[2 * unit - 2] = result[:, :LANES]
            back[2 * unit - 1] = result[:, LANES:]

    for part, out_ref in enumerate((away_ref, keep_ref)):

        def lower(step, carry, out_ref=out_ref, offset=(1 - part) * (windows // 2)):
            at = pl.ds(pl.multiple_of(offset + step * 8, 8), 8)
            b0, b4, b1r, b1i, b2r, b2i, b3r, b3i = (back[u, at, :] for u in range(8))
            scale = powers[at, :]
            plus, minus = (b0 + b4) * 0.5, (b0 - b4) * 0.5
            evens = (plus + b2r, minus - b2i, plus - b2r, minus + b2i)
            u, v = (b1r - b3r) * ROOT_HALF, (b1i + b3i) * ROOT_HALF
            odds = (b1r + b3r, u - v, b3i - b1i, -(u + v))
            for l in range(4):
                out_ref[pl.ds(step * 64 + l, 8, stride=8), :] = 1.0 + (evens[l] + odds[l]) * scale
                out_ref[pl.ds(step * 64 + l + 4, 8, stride=8), :] = 1.0 + (evens[l] - odds[l]) * scale
            return carry

        lax.fori_loop(0, windows // 16, lower, 0, unroll=5)


def band_planes(shifts, fractions, first, second, top, bottom):
    windows = first.shape[0] * first.shape[1] // (WIN * WIN)
    tiles = first.shape[1] // LANES
    tall = first.shape[0] + 2 * HALO

    def pinned(array):
        return pltpu.with_memory_space_constraint(array, pltpu.HBM)

    first, second, *tables = map(pinned, (first, second, *(jnp.asarray(t) for t in dft_tables())))
    vmem = pl.BlockSpec(memory_space=pltpu.VMEM)
    hbm = pl.BlockSpec(memory_space=pltpu.HBM)
    either = pl.BlockSpec(memory_space=pl.ANY)
    f32, bf16 = jnp.float32, jnp.bfloat16
    half = jax.ShapeDtypeStruct((windows * 4, LANES), f32)
    pairs = [
        pltpu.VMEM((2, windows, 2 * LANES), bf16),
        pltpu.VMEM((3, windows, 2 * LANES), bf16),
        pltpu.VMEM((3, windows, 2 * LANES), bf16),
    ]
    held = [pltpu.VMEM(t.shape, bf16) for t in tables]
    spectra, powers = pl.pallas_call(
        first_kernel,
        out_shape=[
            jax.ShapeDtypeStruct((5, windows, 2 * LANES), f32),
            jax.ShapeDtypeStruct((windows, LANES), f32),
        ],
        in_specs=[hbm, hbm, hbm],
        out_specs=[vmem, vmem],
        scratch_shapes=[
            pltpu.VMEM((tiles, first.shape[0], LANES), f32),
            pltpu.VMEM((windows * 8, LANES), f32),
            *pairs,
            *held,
            pltpu.SemaphoreType.DMA((tiles,)),
            pltpu.SemaphoreType.DMA((2,)),
        ],
        compiler_params=pltpu.CompilerParams(vmem_limit_bytes=30 * 1024 * 1024),
        cost_estimate=pl.CostEstimate(flops=10**10, bytes_accessed=2 * 10**7, transcendentals=0),
        name="first_spectra",
    )(first, *tables)
    row_shape = (2, 5, 1, 80)
    return pl.pallas_call(
        band_kernel,
        out_shape=[half, half],
        in_specs=[hbm, hbm, hbm, either, either, hbm, hbm, vmem, vmem],
        out_specs=[vmem, vmem],
        scratch_shapes=[
            pltpu.VMEM((2 * tiles + 1, tall, LANES), f32),
            pltpu.VMEM((2 * tiles + 1, tall, LANES), f32),
            pltpu.VMEM((10, 2, 8, LANES), f32),
            pltpu.VMEM((windows * 8, LANES), f32),
            *pairs,
            pltpu.VMEM((windows, LANES), f32),
            pltpu.VMEM((8, windows, LANES), f32),
            pltpu.VMEM(row_shape, f32),
            pltpu.SMEM(row_shape, jnp.int32),
            pltpu.VMEM((8, 8, LANES), f32),
            pltpu.SMEM((8, 8, LANES), f32),
            *held,
            pltpu.SemaphoreType.DMA((3, tiles)),
            pltpu.SemaphoreType.DMA((5,)),
        ],
        compiler_params=pltpu.CompilerParams(vmem_limit_bytes=40 * 1024 * 1024),
        name="band_planes",
    )(pinned(jnp.swapaxes(shifts, 1, 2)), pinned(jnp.swapaxes(fractions, 1, 2)), second, top, bottom, *tables,
      spectra, powers)


def along_z(array, hops):
    pairs = [(2 * z + c, 2 * ((z + (hops, -hops)[c]) % 8) + c) for z in range(8) for c in range(2)]
    return lax.ppermute(array, "sep", pairs)


def reduced(keep, away):
    size = keep.shape[0] // 8
    parts = keep * lax.ppermute(away, "sep", [(s, s ^ 1) for s in range(16)])
    ahead = along_z(parts[3 * size : 5 * size], 1)
    behind = along_z(parts[5 * size :], -1)
    near = parts[: 3 * size] * behind
    third = along_z(near[size : 2 * size] * ahead[size:], 3)
    sixth = along_z(near[2 * size :], -2)
    return near[:size] * ahead[:size] * third * sixth


def local(first, seconds, shifts, fractions):
    second = seconds[0]
    top = lax.ppermute(second[-HALO:], "tile", [(i, i + 1) for i in range(15)])
    bottom = lax.ppermute(second[:HALO], "tile", [(i + 1, i) for i in range(15)])
    planes = band_planes(shifts, fractions, first, second, top, bottom)
    return reduced(*planes).reshape(5, 5, 1024)


def solution(mesh):
    in_specs = (
        P("tile", None),
        P("sep", "tile", None),
        P(None, "sep", "tile", None),
        P(None, "sep", "tile", None),
    )
    out_specs = P("tile", "sep", None)
    return jax.shard_map(local, mesh=mesh, in_specs=in_specs, out_specs=out_specs, check_vma=False)
```

time: 72.6 us -> 58.2 us (0.80)
  Pallas kernels: 27 us -> 19.7 us
  starting transfers between devices: 22.3 us -> 15.9 us
  waiting for transfers between devices: 18.9 us -> 20.4 us
  local copies, waits for them, and re-layouts: 3.15 us -> 1.74 us
    pallas_call x2, Pallas kernels: 27 us -> 19.7 us  [the longest x1 14 us: band_planes(): pl.pallas_call(band_kernel, out_shape=[half, half], in_specs=[hbm, hbm, h...]
    ppermute x8 -> x4, starting transfers between devices: 14.2 us -> 8.67 us  [along_z(): return lax.ppermute(array, 'sep', pairs)]
    unnamed x6 -> x0, local copies, waits for them, and re-layouts: 2.07 us -> none
    ppermute x1, waiting for transfers between devices: 0.01 us -> 2.06 us  [local(): top = lax.ppermute(second[-HALO:], 'tile', [(i, i + 1) for i in range(15)])]
    ppermute x1, starting transfers between devices: 3.48 us -> 1.92 us  [local(): top = lax.ppermute(second[-HALO:], 'tile', [(i, i + 1) for i in range(15)])]
    ppermute x8 -> x4, waiting for transfers between devices: 17.3 us -> 16 us  [along_z(): return lax.ppermute(array, 'sep', pairs)]
    ppermute x2 -> x1, waiting for transfers between devices: 1.62 us -> 2.32 us  [reduced(): parts = keep * lax.ppermute(away, 'sep', [(s, s ^ 1) for s in range(16)])]
  transfers between devices with their start and end apart: 12 -> 7, of which waited for: 7 -> 5; matrix products, arithmetic and copies ran while one was open for 2% -> 0% of each run, Pallas kernels for 21% -> 10%
where the time goes in v3:
time: 58.2 us; the launch traced here: 58 us
  waiting for transfers between devices  20.4 us (35%)
  Pallas kernels  19.7 us (34%)
  starting transfers between devices  15.9 us (27%)
  local copies, waits for them, and re-layouts  1.74 us (3%)
    ppermute x4, waiting for transfers between devices, along_z(): return lax.ppermute(array, 'sep', pairs)  16 us
    pallas_call x1, Pallas kernels, band_planes(): pl.pallas_call(band_kernel, out_shape=[half, half], in_specs=[hbm, hbm, h...  14 us
    ppermute x4, starting transfers between devices, along_z(): return lax.ppermute(array, 'sep', pairs)  8.67 us
    pallas_call x1, Pallas kernels, band_planes(): pl.pallas_call(first_kernel, out_shape=[jax.ShapeDtypeStruct((5, windows,...  5.66 us
    ppermute x1, starting transfers between devices, local(): lax.ppermute(second[:HALO], 'tile', [(i + 1, i) for i in range(15)])  5.19 us
    ppermute x1, waiting for transfers between devices, reduced(): parts = keep * lax.ppermute(away, 'sep', [(s, s ^ 1) for s in range(16)])  2.32 us
    ppermute x1, waiting for transfers between devices, local(): top = lax.ppermute(second[-HALO:], 'tile', [(i, i + 1) for i in range(15)])  2.06 us
    ppermute x1, starting transfers between devices, local(): top = lax.ppermute(second[-HALO:], 'tile', [(i, i + 1) for i in range(15)])  1.92 us
  transfers between devices with their start and end apart: 7, of which 5 were waited for; matrix products, arithmetic and copies ran while one was open for 0% of the time, Pallas kernels for 10%

profile of v3, /device:TPU:6, one launch (start us, length us, event | category | flops | bytes accessed | tf_op | source)
XLA Modules:
  0.0 58.0 jit_solution(5508064677467966857)
XLA Ops:
  0.0 1.0 %slice_bitcast_fusion = (f32[16,2560]{1,0:T(8,128)S(1)}, f32[16,2560]{1,0:T(8,128)S(1)}) fusion(f32[1,160,2560]{2,1,0:T(8,128)} %param.7), kind=kLoop, calls=%fused_computation.1 | loop fusion | bytes 655360 | tf_op jit(solution)/shard_map/slice | solution.py:400
  1.0 5.2 %collective-permute-start.1 = (f32[16,2560]{1,0:T(8,128)S(1)}, f32[16,2560]{1,0:T(8,128)S(1)}, u32[]{:S(2)}, u32[]{:S(2)}) collective-permute-start(f32[16,2560]{1,0:T(8,128)S(1)} %get-tuple-element.13), channel_id=1, source_target_pairs={{1,0},{2,1},{3,2},{4,3},{5,4},{6,5},{7,6},{8,7},{9,8},{10,9},{11,1... | collective-permute-start | bytes 491528 | tf_op jit(solution)/shard_map/ppermute | solution.py:400
  6.2 1.9 %collective-permute-start = (f32[16,2560]{1,0:T(8,128)S(1)}, f32[16,2560]{1,0:T(8,128)S(1)}, u32[]{:S(2)}, u32[]{:S(2)}) collective-permute-start(f32[16,2560]{1,0:T(8,128)S(1)} %get-tuple-element.14), channel_id=1, source_target_pairs={{0,1},{1,2},{2,3},{3,4},{4,5},{5,6},{6,7},{7,8},{8,9},{9,10},{10,1... | collective-permute-start | bytes 491528 | tf_op jit(solution)/shard_map/ppermute | solution.py:399
  8.1 5.7 %first_spectra.1 = (f32[5,400,256]{2,1,0:T(8,128)S(1)}, f32[400,128]{1,0:T(8,128)S(1)}) custom-call(f32[160,2560]{1,0:T(8,128)} %first_hbm.1, bf16[5,256,256]{2,1,0:T(8,128)(2,1)} %constant.4.clone.high_hbm, bf16[5,256,256]{2,1,0:T(8,128)(2,1)} %constant.5.clone.low_hbm), custom_call_target="tpu_custom_call" | custom-call | flops 10000000000 | bytes 20000000 | tf_op jit(solution)/shard_map/first_spectra/pallas_call | solution.py:333
  13.8 0.0 collective-permute-done.1.bottom_hbm
  13.8 2.1 %collective-permute-done.top_hbm = f32[16,2560]{1,0:T(8,128)S(1)} collective-permute-done((f32[16,2560]{1,0:T(8,128)S(1)}, f32[16,2560]{1,0:T(8,128)S(1)}, u32[]{:S(2)}, u32[]{:S(2)}) %collective-permute-start) | collective-permute-done | bytes 163872 | tf_op jit(solution)/shard_map/ppermute | solution.py:399
  15.9 14.0 %band_planes.1 = (f32[1600,128]{1,0:T(8,128)S(1)}, f32[1600,128]{1,0:T(8,128)S(1)}) custom-call(s32[2,5,1,80]{3,2,1,0:T(1,128)} %bitcast.8, f32[2,5,1,80]{3,2,1,0:T(1,128)} %bitcast.9, f32[160,2560]{1,0:T(8,128)} %bitcast.7, f32[16,2560]{1,0:T(8,128)S(1)} %collective-permute-done.top_hbm, f32[16,2560]{1,0:T(8,128)S(1)} %collective-permute-done.1.bottom_hbm, ...), custom_call_target="tpu_custom_call" | custom-call | tf_op jit(solution)/shard_map/band_planes/pallas_call | solution.py:354
  29.9 0.1 collective-permute-start.2
  30.0 2.3 %collective-permute-done.2 = f32[1600,128]{1,0:T(8,128)S(1)} collective-permute-done((f32[1600,128]{1,0:T(8,128)S(1)}, f32[1600,128]{1,0:T(8,128)S(1)}, u32[]{:S(2)}, u32[]{:S(2)}) %collective-permute-start.2) | collective-permute-done | bytes 819232 | tf_op jit(solution)/shard_map/ppermute | solution.py:388
  32.4 0.1 mul.18
  32.5 5.9 %collective-permute-start.3 = (f32[600,128]{1,0:T(8,128)S(1)}, f32[600,128]{1,0:T(8,128)S(1)}, u32[]{:S(2)}, u32[]{:S(2)}) collective-permute-start(f32[600,128]{1,0:T(8,128)S(1)} %slice.49), channel_id=1, source_target_pairs={{0,224},{16,48},{32,0},{48,80},{64,32},{80,112},{96,64},{112,144},... | collective-permute-start | bytes 921608 | tf_op jit(solution)/shard_map/ppermute | solution.py:383
  38.4 0.1 collective-permute-start.4
  38.5 5.7 %collective-permute-done.3 = f32[600,128]{1,0:T(8,128)S(1)} collective-permute-done((f32[600,128]{1,0:T(8,128)S(1)}, f32[600,128]{1,0:T(8,128)S(1)}, u32[]{:S(2)}, u32[]{:S(2)}) %collective-permute-start.3) | collective-permute-done | bytes 307232 | tf_op jit(solution)/shard_map/ppermute | solution.py:383
  44.3 1.2 %collective-permute-done.4 = f32[400,128]{1,0:T(8,128)S(1)} collective-permute-done((f32[400,128]{1,0:T(8,128)S(1)}, f32[400,128]{1,0:T(8,128)S(1)}, u32[]{:S(2)}, u32[]{:S(2)}) %collective-permute-start.4) | collective-permute-done | bytes 204832 | tf_op jit(solution)/shard_map/ppermute | solution.py:383
  45.5 1.0 %collective-permute-start.5 = (f32[200,128]{1,0:T(8,128)S(1)}, f32[200,128]{1,0:T(8,128)S(1)}, u32[]{:S(2)}, u32[]{:S(2)}) collective-permute-start(f32[200,128]{1,0:T(8,128)S(1)} %get-tuple-element.15), channel_id=1, source_target_pairs={{0,96},{16,176},{32,128},{48,208},{64,160},{80,240},{96,192},{112,... | collective-permute-start | bytes 307208 | tf_op jit(solution)/shard_map/ppermute | solution.py:383
  46.5 1.6 %collective-permute-start.6 = (f32[200,128]{1,0:T(8,128)S(1)}, f32[200,128]{1,0:T(8,128)S(1)}, u32[]{:S(2)}, u32[]{:S(2)}) collective-permute-start(f32[200,128]{1,0:T(8,128)S(1)} %get-tuple-element.16), channel_id=1, source_target_pairs={{0,192},{16,80},{32,224},{48,112},{64,0},{80,144},{96,32},{112,176... | collective-permute-start | bytes 307208 | tf_op jit(solution)/shard_map/ppermute | solution.py:383
  48.2 9.1 %collective-permute-done.5 = f32[200,128]{1,0:T(8,128)S(1)} collective-permute-done((f32[200,128]{1,0:T(8,128)S(1)}, f32[200,128]{1,0:T(8,128)S(1)}, u32[]{:S(2)}, u32[]{:S(2)}) %collective-permute-start.5) | collective-permute-done | bytes 102432 | tf_op jit(solution)/shard_map/ppermute | solution.py:383
  57.3 0.0 collective-permute-done.6
  57.3 0.7 %reshape.5 = f32[5,5,1024]{2,1,0:T(8,128)} reshape(f32[200,128]{1,0:T(8,128)S(1)} %fusion.1) | data formatting | bytes 204800 | tf_op jit(solution)/shard_map/reshape | solution.py:402
  (5 shorter events, 0.1 us)
Async XLA Ops:
  1.0 12.8 %collective-permute-start.1 = (f32[16,2560]{1,0:T(8,128)S(1)}, f32[16,2560]{1,0:T(8,128)S(1)}, u32[]{:S(2)}, u32[]{:S(2)}) collective-permute-start(f32[16,2560]{1,0:T(8,128)S(1)} %get-tuple-element.13), channel_id=1, source_target_pairs={{1,0},{2,1},{3,2},{4,3},{5,4},{6,5},{7,6},{8,7},{9,8},{10,9},{11,1... | collective-permute-start | bytes 491528 | tf_op jit(solution)/shard_map/ppermute | solution.py:400
  6.2 9.7 %collective-permute-start = (f32[16,2560]{1,0:T(8,128)S(1)}, f32[16,2560]{1,0:T(8,128)S(1)}, u32[]{:S(2)}, u32[]{:S(2)}) collective-permute-start(f32[16,2560]{1,0:T(8,128)S(1)} %get-tuple-element.14), channel_id=1, source_target_pairs={{0,1},{1,2},{2,3},{3,4},{4,5},{5,6},{6,7},{7,8},{8,9},{9,10},{10,1... | collective-permute-start | bytes 491528 | tf_op jit(solution)/shard_map/ppermute | solution.py:399
  29.9 2.4 %collective-permute-start.2 = (f32[1600,128]{1,0:T(8,128)S(1)}, f32[1600,128]{1,0:T(8,128)S(1)}, u32[]{:S(2)}, u32[]{:S(2)}) collective-permute-start(f32[1600,128]{1,0:T(8,128)S(1)} %get-tuple-element.12), channel_id=1, source_target_pairs={{0,16},{16,0},{32,48},{48,32},{64,80},{80,64},{96,112},{112,96},{1... | collective-permute-start | bytes 2457608 | tf_op jit(solution)/shard_map/ppermute | solution.py:388
  32.5 11.8 %collective-permute-start.3 = (f32[600,128]{1,0:T(8,128)S(1)}, f32[600,128]{1,0:T(8,128)S(1)}, u32[]{:S(2)}, u32[]{:S(2)}) collective-permute-start(f32[600,128]{1,0:T(8,128)S(1)} %slice.49), channel_id=1, source_target_pairs={{0,224},{16,48},{32,0},{48,80},{64,32},{80,112},{96,64},{112,144},... | collective-permute-start | bytes 921608 | tf_op jit(solution)/shard_map/ppermute | solution.py:383
  38.4 7.0 %collective-permute-start.4 = (f32[400,128]{1,0:T(8,128)S(1)}, f32[400,128]{1,0:T(8,128)S(1)}, u32[]{:S(2)}, u32[]{:S(2)}) collective-permute-start(f32[400,128]{1,0:T(8,128)S(1)} %slice.51), channel_id=1, source_target_pairs={{0,32},{16,240},{32,64},{48,16},{64,96},{80,48},{96,128},{112,80},... | collective-permute-start | bytes 614408 | tf_op jit(solution)/shard_map/ppermute | solution.py:383
  45.5 11.7 %collective-permute-start.5 = (f32[200,128]{1,0:T(8,128)S(1)}, f32[200,128]{1,0:T(8,128)S(1)}, u32[]{:S(2)}, u32[]{:S(2)}) collective-permute-start(f32[200,128]{1,0:T(8,128)S(1)} %get-tuple-element.15), channel_id=1, source_target_pairs={{0,96},{16,176},{32,128},{48,208},{64,160},{80,240},{96,192},{112,... | collective-permute-start | bytes 307208 | tf_op jit(solution)/shard_map/ppermute | solution.py:383
  46.5 10.7 %collective-permute-start.6 = (f32[200,128]{1,0:T(8,128)S(1)}, f32[200,128]{1,0:T(8,128)S(1)}, u32[]{:S(2)}, u32[]{:S(2)}) collective-permute-start(f32[200,128]{1,0:T(8,128)S(1)} %get-tuple-element.16), channel_id=1, source_target_pairs={{0,192},{16,80},{32,224},{48,112},{64,0},{80,144},{96,32},{112,176... | collective-permute-start | bytes 307208 | tf_op jit(solution)/shard_map/ppermute | solution.py:383

commit v4 on v3

--- a/solution.py
+++ b/solution.py
@@ -112,7 +112,7 @@
     return dot(pair_hi[unit - 2], hi) + dot(pair_lo[unit - 2], hi) + dot(pair_hi[unit - 2], lo)
 
 
-def first_kernel(first_hbm, high_hbm, low_hbm, spectra_ref, power_ref,
+def first_kernel(fraction_hbm, first_hbm, high_hbm, low_hbm, spectra_ref, power_ref, taps_ref, fraction_ref,
                  first, first_win, pair_ends, pair_hi, pair_lo, table_hi, table_lo, first_sems, table_sems):
     win_rows = first_hbm.shape[0] // WIN
     block = first_win.shape[0] // 8 // BLOCKS
@@ -125,9 +125,11 @@
     table_copies = [
         pltpu.make_async_copy(high_hbm, table_hi, table_sems.at[0]),
         pltpu.make_async_copy(low_hbm, table_lo, table_sems.at[1]),
+        pltpu.make_async_copy(fraction_hbm, fraction_ref, table_sems.at[2]),
     ]
     for copy in first_copies + table_copies:
         copy.start()
+    taps_ref[...] = jnp.zeros_like(taps_ref)
     for copy in first_copies:
         copy.wait()
 
@@ -151,7 +153,7 @@
                     first_win[pl.ds(pl.multiple_of(base[k // 5] + (k % 5) * 8, 8), 8), :] = value
         return carry
 
-    lax.fori_loop(0, 4 * win_rows, gather, 0, unroll=2)
+    lax.fori_loop(0, 4 * win_rows, gather, 0, unroll=4)
 
 
     def finish(at, power):
@@ -160,71 +162,59 @@
     lift_windows(first_win, pair_ends, pair_hi, pair_lo, finish)
     for copy in table_copies:
         copy.wait()
+    for axis in range(2):
+        for a, values in enumerate(cubic_weights(fraction_ref[axis, :, 0, :])):
+            taps_ref[2 * a + axis, 0:5, 0:80] = values
     for unit in range(5):
         spectra_ref[unit] = spectrum_of(unit, pair_ends, pair_hi, pair_lo, table_hi, table_lo)
 
 
-def band_kernel(shift_hbm, fraction_hbm, second_hbm, top_hbm, bottom_hbm, high_hbm, low_hbm, spectra_ref, power_ref,
+def band_kernel(shift_hbm, taps_vmem, second_ref, top_ref, bottom_ref, high_hbm, low_hbm, spectra_ref, power_ref,
                 keep_ref, away_ref, frame, swapped, shifted, second_win,
-                pair_ends, pair_hi, pair_lo, powers, back, fraction_ref, shift_ref, taps_vmem, taps_ref,
-                table_hi, table_lo, frame_sems, small_sems):
+                pair_ends, pair_hi, pair_lo, powers, back, shift_ref, taps_ref, table_hi, table_lo, small_sems):
     windows = second_win.shape[0] // 8
-    band = second_hbm.shape[0]
+    band = second_ref.shape[0]
     win_rows = band // WIN
     block = windows // BLOCKS
-    tiles = second_hbm.shape[1] // LANES
+    tiles = second_ref.shape[1] // LANES
     lane, low_half, even = masks()
 
     small_copies = [
-        pltpu.make_async_copy(fraction_hbm, fraction_ref, small_sems.at[0]),
+        pltpu.make_async_copy(taps_vmem, taps_ref, small_sems.at[0]),
         pltpu.make_async_copy(shift_hbm, shift_ref, small_sems.at[1]),
     ]
     table_copies = [
         pltpu.make_async_copy(high_hbm, table_hi, small_sems.at[2]),
         pltpu.make_async_copy(low_hbm, table_lo, small_sems.at[3]),
     ]
-    frame_copies = [
-        pltpu.make_async_copy(
-            ref.at[:, pl.ds(g * LANES, LANES)],
-            frame.at[2 * g + 1, pl.ds(row, rows), :],
-            frame_sems.at[n, g],
-        )
-        for n, (ref, row, rows) in enumerate(
-            ((second_hbm, HALO, band), (top_hbm, 0, HALO), (bottom_hbm, HALO + band, HALO))
-        )
-        for g in range(tiles)
-    ]
-    for copy in small_copies + frame_copies + table_copies:
+    for copy in small_copies + table_copies:
         copy.start()
 
-    for copy in small_copies:
-        copy.wait()
-    for axis in range(2):
-        for a, values in enumerate(cubic_weights(fraction_ref[axis, :, 0, :])):
-            taps_vmem[2 * a + axis, 0:5, 0:80] = values
-    taps_copy = pltpu.make_async_copy(taps_vmem, taps_ref, small_sems.at[4])
-    taps_copy.start()
-
-    for copy in frame_copies:
-        copy.wait()
     wide = lax.broadcasted_iota(jnp.int32, (16, LANES), 1) < 64
 
-    def fill(step, carry):
-        rows = pl.ds(pl.multiple_of(step * 16, 16), 16)
+    def fill(source, source_row, row):
+        rows = pl.ds(pl.multiple_of(row, 16), 16)
         before = before_turned = jnp.zeros((16, LANES), jnp.float32)
         for g in range(tiles):
-            here = frame[2 * g + 1, rows, :]
+            here = source[pl.ds(pl.multiple_of(source_row, 16), 16), g * LANES : (g + 1) * LANES]
             turned = pltpu.roll(here, 64, 1)
+            frame[2 * g + 1, rows, :] = here
             swapped[2 * g + 1, rows, :] = turned
             frame[2 * g, rows, :] = jnp.where(wide, before_turned, turned)
             swapped[2 * g, rows, :] = jnp.where(wide, here, before)
             before, before_turned = here, turned
         frame[2 * tiles, rows, :] = jnp.where(wide, before_turned, 0.0)
         swapped[2 * tiles, rows, :] = jnp.where(wide, 0.0, before)
+
+    def fill_band(step, carry):
+        fill(second_ref, step * 16, step * 16 + HALO)
         return carry
 
-    lax.fori_loop(0, frame.shape[1] // 16, fill, 0)
-    taps_copy.wait()
+    fill(top_ref, 0, 0)
+    fill(bottom_ref, 0, HALO + band)
+    lax.fori_loop(0, band // 16, fill_band, 0, unroll=2)
+    for copy in small_copies:
+        copy.wait()
 
     def mix_rows(step, k):
         i, column = step >> 3, (step & 7) * 10 + k
@@ -265,7 +255,7 @@
             mix_rows(later, k)
         return carry
 
-    lax.fori_loop(0, steps, deform, 0)
+    lax.fori_loop(0, steps, deform, 0, unroll=2)
 
     def finish(at, power):
         scale = (2.0 / (1024.0 * 1024.0)) / jnp.sqrt(power_ref[at, :] * power)
@@ -318,10 +308,9 @@
     def pinned(array):
         return pltpu.with_memory_space_constraint(array, pltpu.HBM)
 
-    first, second, *tables = map(pinned, (first, second, *(jnp.asarray(t) for t in dft_tables())))
+    tables = [jnp.asarray(t) for t in dft_tables()]
     vmem = pl.BlockSpec(memory_space=pltpu.VMEM)
     hbm = pl.BlockSpec(memory_space=pltpu.HBM)
-    either = pl.BlockSpec(memory_space=pl.ANY)
     f32, bf16 = jnp.float32, jnp.bfloat16
     half = jax.ShapeDtypeStruct((windows * 4, LANES), f32)
     pairs = [
@@ -330,31 +319,33 @@
         pltpu.VMEM((3, windows, 2 * LANES), bf16),
     ]
     held = [pltpu.VMEM(t.shape, bf16) for t in tables]
-    spectra, powers = pl.pallas_call(
+    row_shape = (2, 5, 1, 80)
+    spectra, powers, taps = pl.pallas_call(
         first_kernel,
         out_shape=[
             jax.ShapeDtypeStruct((5, windows, 2 * LANES), f32),
             jax.ShapeDtypeStruct((windows, LANES), f32),
+            jax.ShapeDtypeStruct((8, 8, LANES), f32),
         ],
-        in_specs=[hbm, hbm, hbm],
-        out_specs=[vmem, vmem],
+        in_specs=[hbm, hbm, hbm, hbm],
+        out_specs=[vmem, vmem, vmem],
         scratch_shapes=[
+            pltpu.VMEM(row_shape, f32),
             pltpu.VMEM((tiles, first.shape[0], LANES), f32),
             pltpu.VMEM((windows * 8, LANES), f32),
             *pairs,
             *held,
             pltpu.SemaphoreType.DMA((tiles,)),
-            pltpu.SemaphoreType.DMA((2,)),
+            pltpu.SemaphoreType.DMA((3,)),
         ],
         compiler_params=pltpu.CompilerParams(vmem_limit_bytes=30 * 1024 * 1024),
         cost_estimate=pl.CostEstimate(flops=10**10, bytes_accessed=2 * 10**7, transcendentals=0),
         name="first_spectra",
-    )(first, *tables)
-    row_shape = (2, 5, 1, 80)
+    )(pinned(jnp.swapaxes(fractions, 1, 2)), pinned(first), *map(pinned, tables))
     return pl.pallas_call(
         band_kernel,
         out_shape=[half, half],
-        in_specs=[hbm, hbm, hbm, either, either, hbm, hbm, vmem, vmem],
+        in_specs=[hbm, vmem, vmem, vmem, vmem, hbm, hbm, vmem, vmem],
         out_specs=[vmem, vmem],
         scratch_shapes=[
             pltpu.VMEM((2 * tiles + 1, tall, LANES), f32),
@@ -364,18 +355,15 @@
             *pairs,
             pltpu.VMEM((windows, LANES), f32),
             pltpu.VMEM((8, windows, LANES), f32),
-            pltpu.VMEM(row_shape, f32),
             pltpu.SMEM(row_shape, jnp.int32),
-            pltpu.VMEM((8, 8, LANES), f32),
             pltpu.SMEM((8, 8, LANES), f32),
             *held,
-            pltpu.SemaphoreType.DMA((3, tiles)),
-            pltpu.SemaphoreType.DMA((5,)),
+            pltpu.SemaphoreType.DMA((4,)),
         ],
         compiler_params=pltpu.CompilerParams(vmem_limit_bytes=40 * 1024 * 1024),
         name="band_planes",
-    )(pinned(jnp.swapaxes(shifts, 1, 2)), pinned(jnp.swapaxes(fractions, 1, 2)), second, top, bottom, *tables,
-      spectra, powers)
+    )(pinned(jnp.swapaxes(shifts, 1, 2)), taps, second, top, bottom,
+      *map(pinned, tables), spectra, powers)
 
 
 def along_z(array, hops):

time: 58.2 us -> 55.5 us (0.954)
  Pallas kernels: 19.7 us -> 16.6 us
    pallas_call x1, Pallas kernels: 14 us -> 11.3 us  [band_planes(): pl.pallas_call(band_kernel, out_shape=[half, half], in_specs=[hbm, vmem,...]
where the time goes in v4:
time: 55.5 us; the launch traced here: 55.3 us
  waiting for transfers between devices  20.8 us (37%)
  Pallas kernels  16.6 us (30%)
  starting transfers between devices  15.9 us (29%)
  local copies, waits for them, and re-layouts  1.74 us (3%)
    ppermute x4, waiting for transfers between devices, along_z(): return lax.ppermute(array, 'sep', pairs)  16 us
    pallas_call x1, Pallas kernels, band_planes(): pl.pallas_call(band_kernel, out_shape=[half, half], in_specs=[hbm, vmem,...  11.3 us
    ppermute x4, starting transfers between devices, along_z(): return lax.ppermute(array, 'sep', pairs)  8.66 us
    pallas_call x1, Pallas kernels, band_planes(): pl.pallas_call(first_kernel, out_shape=[jax.ShapeDtypeStruct((5, windows,...  5.29 us
    ppermute x1, starting transfers between devices, local(): lax.ppermute(second[:HALO], 'tile', [(i + 1, i) for i in range(15)])  5.19 us
    ppermute x1, waiting for transfers between devices, local(): top = lax.ppermute(second[-HALO:], 'tile', [(i, i + 1) for i in range(15)])  2.41 us
    ppermute x1, waiting for transfers between devices, reduced(): parts = keep * lax.ppermute(away, 'sep', [(s, s ^ 1) for s in range(16)])  2.32 us
    ppermute x1, starting transfers between devices, local(): top = lax.ppermute(second[-HALO:], 'tile', [(i, i + 1) for i in range(15)])  1.92 us
  transfers between devices with their start and end apart: 7, of which 5 were waited for; matrix products, arithmetic and copies ran while one was open for 0% of the time, Pallas kernels for 10%

profile of v4, /device:TPU:6, one launch (start us, length us, event | category | flops | bytes accessed | tf_op | source)
XLA Modules:
  0.0 55.3 jit_solution(15496308492315232440)
XLA Ops:
  0.0 1.0 %slice_bitcast_fusion = (f32[16,2560]{1,0:T(8,128)S(1)}, f32[16,2560]{1,0:T(8,128)S(1)}) fusion(f32[1,160,2560]{2,1,0:T(8,128)} %param.7), kind=kLoop, calls=%fused_computation.1 | loop fusion | bytes 655360 | tf_op jit(solution)/shard_map/slice | solution.py:388
  1.0 5.2 %collective-permute-start.1 = (f32[16,2560]{1,0:T(8,128)S(1)}, f32[16,2560]{1,0:T(8,128)S(1)}, u32[]{:S(2)}, u32[]{:S(2)}) collective-permute-start(f32[16,2560]{1,0:T(8,128)S(1)} %get-tuple-element.15), channel_id=1, source_target_pairs={{1,0},{2,1},{3,2},{4,3},{5,4},{6,5},{7,6},{8,7},{9,8},{10,9},{11,1... | collective-permute-start | bytes 491528 | tf_op jit(solution)/shard_map/ppermute | solution.py:388
  6.2 1.9 %collective-permute-start = (f32[16,2560]{1,0:T(8,128)S(1)}, f32[16,2560]{1,0:T(8,128)S(1)}, u32[]{:S(2)}, u32[]{:S(2)}) collective-permute-start(f32[16,2560]{1,0:T(8,128)S(1)} %get-tuple-element.16), channel_id=1, source_target_pairs={{0,1},{1,2},{2,3},{3,4},{4,5},{5,6},{6,7},{7,8},{8,9},{9,10},{10,1... | collective-permute-start | bytes 491528 | tf_op jit(solution)/shard_map/ppermute | solution.py:387
  8.1 0.0 copy-start
  8.2 5.3 %first_spectra.1 = (f32[5,400,256]{2,1,0:T(8,128)S(1)}, f32[400,128]{1,0:T(8,128)S(1)}, f32[8,8,128]{2,1,0:T(8,128)S(1)}) custom-call(f32[2,5,1,80]{3,2,1,0:T(1,128)} %bitcast.9, f32[160,2560]{1,0:T(8,128)} %first_hbm.1, bf16[5,256,256]{2,1,0:T(8,128)(2,1)} %constant.4.clone.high_hbm, bf16[5,256,256]{2,1,0:T(8,128)(2,1)} %constant.5.clone.low_hbm), custom_call_target="tpu_custom_call" | custom-call | flops 10000000000 | bytes 20000000 | tf_op jit(solution)/shard_map/first_spectra/pallas_call | solution.py:323
  13.5 0.0 collective-permute-done.1.bottom_ref
  13.5 2.4 %collective-permute-done.top_ref = f32[16,2560]{1,0:T(8,128)S(1)} collective-permute-done((f32[16,2560]{1,0:T(8,128)S(1)}, f32[16,2560]{1,0:T(8,128)S(1)}, u32[]{:S(2)}, u32[]{:S(2)}) %collective-permute-start) | collective-permute-done | bytes 163872 | tf_op jit(solution)/shard_map/ppermute | solution.py:387
  15.9 0.0 copy-done
  15.9 11.3 %band_planes.1 = (f32[1600,128]{1,0:T(8,128)S(1)}, f32[1600,128]{1,0:T(8,128)S(1)}) custom-call(s32[2,5,1,80]{3,2,1,0:T(1,128)} %bitcast.8, f32[8,8,128]{2,1,0:T(8,128)S(1)} %get-tuple-element.10.taps_vmem, f32[160,2560]{1,0:T(8,128)S(1)} %bitcast.7, f32[16,2560]{1,0:T(8,128)S(1)} %collective-permute-done.top_ref, ...), custom_call_target="tpu_custom_call" | custom-call | tf_op jit(solution)/shard_map/band_planes/pallas_call | solution.py:345
  27.2 0.1 collective-permute-start.2
  27.3 2.3 %collective-permute-done.2 = f32[1600,128]{1,0:T(8,128)S(1)} collective-permute-done((f32[1600,128]{1,0:T(8,128)S(1)}, f32[1600,128]{1,0:T(8,128)S(1)}, u32[]{:S(2)}, u32[]{:S(2)}) %collective-permute-start.2) | collective-permute-done | bytes 819232 | tf_op jit(solution)/shard_map/ppermute | solution.py:376
  29.7 0.1 mul.18
  29.8 5.9 %collective-permute-start.3 = (f32[600,128]{1,0:T(8,128)S(1)}, f32[600,128]{1,0:T(8,128)S(1)}, u32[]{:S(2)}, u32[]{:S(2)}) collective-permute-start(f32[600,128]{1,0:T(8,128)S(1)} %slice.49), channel_id=1, source_target_pairs={{0,224},{16,48},{32,0},{48,80},{64,32},{80,112},{96,64},{112,144},... | collective-permute-start | bytes 921608 | tf_op jit(solution)/shard_map/ppermute | solution.py:371
  35.7 0.1 collective-permute-start.4
  35.8 5.7 %collective-permute-done.3 = f32[600,128]{1,0:T(8,128)S(1)} collective-permute-done((f32[600,128]{1,0:T(8,128)S(1)}, f32[600,128]{1,0:T(8,128)S(1)}, u32[]{:S(2)}, u32[]{:S(2)}) %collective-permute-start.3) | collective-permute-done | bytes 307232 | tf_op jit(solution)/shard_map/ppermute | solution.py:371
  41.6 1.2 %collective-permute-done.4 = f32[400,128]{1,0:T(8,128)S(1)} collective-permute-done((f32[400,128]{1,0:T(8,128)S(1)}, f32[400,128]{1,0:T(8,128)S(1)}, u32[]{:S(2)}, u32[]{:S(2)}) %collective-permute-start.4) | collective-permute-done | bytes 204832 | tf_op jit(solution)/shard_map/ppermute | solution.py:371
  42.8 1.0 %collective-permute-start.5 = (f32[200,128]{1,0:T(8,128)S(1)}, f32[200,128]{1,0:T(8,128)S(1)}, u32[]{:S(2)}, u32[]{:S(2)}) collective-permute-start(f32[200,128]{1,0:T(8,128)S(1)} %get-tuple-element.17), channel_id=1, source_target_pairs={{0,96},{16,176},{32,128},{48,208},{64,160},{80,240},{96,192},{112,... | collective-permute-start | bytes 307208 | tf_op jit(solution)/shard_map/ppermute | solution.py:371
  43.8 1.6 %collective-permute-start.6 = (f32[200,128]{1,0:T(8,128)S(1)}, f32[200,128]{1,0:T(8,128)S(1)}, u32[]{:S(2)}, u32[]{:S(2)}) collective-permute-start(f32[200,128]{1,0:T(8,128)S(1)} %get-tuple-element.18), channel_id=1, source_target_pairs={{0,192},{16,80},{32,224},{48,112},{64,0},{80,144},{96,32},{112,176... | collective-permute-start | bytes 307208 | tf_op jit(solution)/shard_map/ppermute | solution.py:371
  45.5 9.1 %collective-permute-done.5 = f32[200,128]{1,0:T(8,128)S(1)} collective-permute-done((f32[200,128]{1,0:T(8,128)S(1)}, f32[200,128]{1,0:T(8,128)S(1)}, u32[]{:S(2)}, u32[]{:S(2)}) %collective-permute-start.5) | collective-permute-done | bytes 102432 | tf_op jit(solution)/shard_map/ppermute | solution.py:371
  54.6 0.0 collective-permute-done.6
  54.6 0.7 %reshape.5 = f32[5,5,1024]{2,1,0:T(8,128)} reshape(f32[200,128]{1,0:T(8,128)S(1)} %fusion.1) | data formatting | bytes 204800 | tf_op jit(solution)/shard_map/reshape | solution.py:390
  (5 shorter events, 0.1 us)
Async XLA Ops:
  1.0 12.4 %collective-permute-start.1 = (f32[16,2560]{1,0:T(8,128)S(1)}, f32[16,2560]{1,0:T(8,128)S(1)}, u32[]{:S(2)}, u32[]{:S(2)}) collective-permute-start(f32[16,2560]{1,0:T(8,128)S(1)} %get-tuple-element.15), channel_id=1, source_target_pairs={{1,0},{2,1},{3,2},{4,3},{5,4},{6,5},{7,6},{8,7},{9,8},{10,9},{11,1... | collective-permute-start | bytes 491528 | tf_op jit(solution)/shard_map/ppermute | solution.py:388
  6.2 9.7 %collective-permute-start = (f32[16,2560]{1,0:T(8,128)S(1)}, f32[16,2560]{1,0:T(8,128)S(1)}, u32[]{:S(2)}, u32[]{:S(2)}) collective-permute-start(f32[16,2560]{1,0:T(8,128)S(1)} %get-tuple-element.16), channel_id=1, source_target_pairs={{0,1},{1,2},{2,3},{3,4},{4,5},{5,6},{6,7},{7,8},{8,9},{9,10},{10,1... | collective-permute-start | bytes 491528 | tf_op jit(solution)/shard_map/ppermute | solution.py:387
  8.1 7.7 %copy-start = (f32[1,160,2560]{2,1,0:T(8,128)S(1)}, f32[1,160,2560]{2,1,0:T(8,128)}, u32[]{:S(2)}) copy-start(f32[1,160,2560]{2,1,0:T(8,128)} %param.7) | copy-start | bytes 4915204
  27.2 2.4 %collective-permute-start.2 = (f32[1600,128]{1,0:T(8,128)S(1)}, f32[1600,128]{1,0:T(8,128)S(1)}, u32[]{:S(2)}, u32[]{:S(2)}) collective-permute-start(f32[1600,128]{1,0:T(8,128)S(1)} %get-tuple-element.14), channel_id=1, source_target_pairs={{0,16},{16,0},{32,48},{48,32},{64,80},{80,64},{96,112},{112,96},{1... | collective-permute-start | bytes 2457608 | tf_op jit(solution)/shard_map/ppermute | solution.py:376
  29.8 11.8 %collective-permute-start.3 = (f32[600,128]{1,0:T(8,128)S(1)}, f32[600,128]{1,0:T(8,128)S(1)}, u32[]{:S(2)}, u32[]{:S(2)}) collective-permute-start(f32[600,128]{1,0:T(8,128)S(1)} %slice.49), channel_id=1, source_target_pairs={{0,224},{16,48},{32,0},{48,80},{64,32},{80,112},{96,64},{112,144},... | collective-permute-start | bytes 921608 | tf_op jit(solution)/shard_map/ppermute | solution.py:371
  35.7 7.0 %collective-permute-start.4 = (f32[400,128]{1,0:T(8,128)S(1)}, f32[400,128]{1,0:T(8,128)S(1)}, u32[]{:S(2)}, u32[]{:S(2)}) collective-permute-start(f32[400,128]{1,0:T(8,128)S(1)} %slice.51), channel_id=1, source_target_pairs={{0,32},{16,240},{32,64},{48,16},{64,96},{80,48},{96,128},{112,80},... | collective-permute-start | bytes 614408 | tf_op jit(solution)/shard_map/ppermute | solution.py:371
  42.8 11.8 %collective-permute-start.5 = (f32[200,128]{1,0:T(8,128)S(1)}, f32[200,128]{1,0:T(8,128)S(1)}, u32[]{:S(2)}, u32[]{:S(2)}) collective-permute-start(f32[200,128]{1,0:T(8,128)S(1)} %get-tuple-element.17), channel_id=1, source_target_pairs={{0,96},{16,176},{32,128},{48,208},{64,160},{80,240},{96,192},{112,... | collective-permute-start | bytes 307208 | tf_op jit(solution)/shard_map/ppermute | solution.py:371
  43.8 10.7 %collective-permute-start.6 = (f32[200,128]{1,0:T(8,128)S(1)}, f32[200,128]{1,0:T(8,128)S(1)}, u32[]{:S(2)}, u32[]{:S(2)}) collective-permute-start(f32[200,128]{1,0:T(8,128)S(1)} %get-tuple-element.18), channel_id=1, source_target_pairs={{0,192},{16,80},{32,224},{48,112},{64,0},{80,144},{96,32},{112,176... | collective-permute-start | bytes 307208 | tf_op jit(solution)/shard_map/ppermute | solution.py:371

commit v5 on v4

--- a/solution.py
+++ b/solution.py
@@ -12,6 +12,7 @@
 
 WIN = 32
 HALO = 16
+SENT = 10
 EPS = 1e-06
 LANES = 128
 BLOCKS = 16
@@ -190,13 +191,11 @@
     for copy in small_copies + table_copies:
         copy.start()
 
-    wide = lax.broadcasted_iota(jnp.int32, (16, LANES), 1) < 64
-
-    def fill(source, source_row, row):
-        rows = pl.ds(pl.multiple_of(row, 16), 16)
-        before = before_turned = jnp.zeros((16, LANES), jnp.float32)
+    def fill(source, source_rows, rows):
+        wide = lax.broadcasted_iota(jnp.int32, (rows.size, LANES), 1) < 64
+        before = before_turned = jnp.zeros((rows.size, LANES), jnp.float32)
         for g in range(tiles):
-            here = source[pl.ds(pl.multiple_of(source_row, 16), 16), g * LANES : (g + 1) * LANES]
+            here = source[source_rows, g * LANES : (g + 1) * LANES]
             turned = pltpu.roll(here, 64, 1)
             frame[2 * g + 1, rows, :] = here
             swapped[2 * g + 1, rows, :] = turned
@@ -207,11 +206,13 @@
         swapped[2 * tiles, rows, :] = jnp.where(wide, 0.0, before)
 
     def fill_band(step, carry):
-        fill(second_ref, step * 16, step * 16 + HALO)
+        row = pl.multiple_of(step * 16, 16)
+        fill(second_ref, pl.ds(row, 16), pl.ds(row + HALO, 16))
         return carry
 
-    fill(top_ref, 0, 0)
-    fill(bottom_ref, 0, HALO + band)
+    sent = top_ref.shape[0]
+    fill(top_ref, pl.ds(0, sent), pl.ds(HALO - sent, sent))
+    fill(bottom_ref, pl.ds(0, sent), pl.ds(HALO + band, sent))
     lax.fori_loop(0, band // 16, fill_band, 0, unroll=2)
     for copy in small_copies:
         copy.wait()
@@ -384,8 +385,8 @@
 
 def local(first, seconds, shifts, fractions):
     second = seconds[0]
-    top = lax.ppermute(second[-HALO:], "tile", [(i, i + 1) for i in range(15)])
-    bottom = lax.ppermute(second[:HALO], "tile", [(i + 1, i) for i in range(15)])
+    top = lax.ppermute(second[-SENT:], "tile", [(i, i + 1) for i in range(15)])
+    bottom = lax.ppermute(second[:SENT], "tile", [(i + 1, i) for i in range(15)])
     planes = band_planes(shifts, fractions, first, second, top, bottom)
     return reduced(*planes).reshape(5, 5, 1024)
 

time: 55.5 us -> 55.5 us (level)
  no operation moved by 1% of the time
where the time goes in v5:
time: 55.5 us; the launch traced here: 55.3 us
  waiting for transfers between devices  20.8 us (37%)
  Pallas kernels  16.6 us (30%)
  starting transfers between devices  15.9 us (29%)
  local copies, waits for them, and re-layouts  1.74 us (3%)
    ppermute x4, waiting for transfers between devices, along_z(): return lax.ppermute(array, 'sep', pairs)  16 us
    pallas_call x1, Pallas kernels, band_planes(): pl.pallas_call(band_kernel, out_shape=[half, half], in_specs=[hbm, vmem,...  11.3 us
    ppermute x4, starting transfers between devices, along_z(): return lax.ppermute(array, 'sep', pairs)  8.67 us
    pallas_call x1, Pallas kernels, band_planes(): pl.pallas_call(first_kernel, out_shape=[jax.ShapeDtypeStruct((5, windows,...  5.28 us
    ppermute x1, starting transfers between devices, local(): lax.ppermute(second[:SENT], 'tile', [(i + 1, i) for i in range(15)])  5.19 us
    ppermute x1, waiting for transfers between devices, local(): top = lax.ppermute(second[-SENT:], 'tile', [(i, i + 1) for i in range(15)])  2.42 us
    ppermute x1, waiting for transfers between devices, reduced(): parts = keep * lax.ppermute(away, 'sep', [(s, s ^ 1) for s in range(16)])  2.32 us
    ppermute x1, starting transfers between devices, local(): top = lax.ppermute(second[-SENT:], 'tile', [(i, i + 1) for i in range(15)])  1.92 us
  transfers between devices with their start and end apart: 7, of which 5 were waited for; matrix products, arithmetic and copies ran while one was open for 0% of the time, Pallas kernels for 10%

profile of v5, /device:TPU:6, one launch (start us, length us, event | category | flops | bytes accessed | tf_op | source)
XLA Modules:
  0.0 55.3 jit_solution(16277947155414494330)
XLA Ops:
  0.0 1.0 %slice_bitcast_fusion = (f32[10,2560]{1,0:T(8,128)S(1)}, f32[10,2560]{1,0:T(8,128)S(1)}) fusion(f32[1,160,2560]{2,1,0:T(8,128)} %param.7), kind=kLoop, calls=%fused_computation.1 | loop fusion | bytes 409600 | tf_op jit(solution)/shard_map/slice | solution.py:389
  1.0 5.2 %collective-permute-start.1 = (f32[10,2560]{1,0:T(8,128)S(1)}, f32[10,2560]{1,0:T(8,128)S(1)}, u32[]{:S(2)}, u32[]{:S(2)}) collective-permute-start(f32[10,2560]{1,0:T(8,128)S(1)} %get-tuple-element.15), channel_id=1, source_target_pairs={{1,0},{2,1},{3,2},{4,3},{5,4},{6,5},{7,6},{8,7},{9,8},{10,9},{11,1... | collective-permute-start | bytes 307208 | tf_op jit(solution)/shard_map/ppermute | solution.py:389
  6.2 1.9 %collective-permute-start = (f32[10,2560]{1,0:T(8,128)S(1)}, f32[10,2560]{1,0:T(8,128)S(1)}, u32[]{:S(2)}, u32[]{:S(2)}) collective-permute-start(f32[10,2560]{1,0:T(8,128)S(1)} %get-tuple-element.16), channel_id=1, source_target_pairs={{0,1},{1,2},{2,3},{3,4},{4,5},{5,6},{6,7},{7,8},{8,9},{9,10},{10,1... | collective-permute-start | bytes 307208 | tf_op jit(solution)/shard_map/ppermute | solution.py:388
  8.1 0.0 copy-start
  8.2 5.3 %first_spectra.1 = (f32[5,400,256]{2,1,0:T(8,128)S(1)}, f32[400,128]{1,0:T(8,128)S(1)}, f32[8,8,128]{2,1,0:T(8,128)S(1)}) custom-call(f32[2,5,1,80]{3,2,1,0:T(1,128)} %bitcast.9, f32[160,2560]{1,0:T(8,128)} %first_hbm.1, bf16[5,256,256]{2,1,0:T(8,128)(2,1)} %constant.4.clone.high_hbm, bf16[5,256,256]{2,1,0:T(8,128)(2,1)} %constant.5.clone.low_hbm), custom_call_target="tpu_custom_call" | custom-call | flops 10000000000 | bytes 20000000 | tf_op jit(solution)/shard_map/first_spectra/pallas_call | solution.py:324
  13.4 0.0 collective-permute-done.1.bottom_ref
  13.5 2.4 %collective-permute-done.top_ref = f32[10,2560]{1,0:T(8,128)S(1)} collective-permute-done((f32[10,2560]{1,0:T(8,128)S(1)}, f32[10,2560]{1,0:T(8,128)S(1)}, u32[]{:S(2)}, u32[]{:S(2)}) %collective-permute-start) | collective-permute-done | bytes 102432 | tf_op jit(solution)/shard_map/ppermute | solution.py:388
  15.9 0.0 copy-done
  15.9 11.3 %band_planes.1 = (f32[1600,128]{1,0:T(8,128)S(1)}, f32[1600,128]{1,0:T(8,128)S(1)}) custom-call(s32[2,5,1,80]{3,2,1,0:T(1,128)} %bitcast.8, f32[8,8,128]{2,1,0:T(8,128)S(1)} %get-tuple-element.10.taps_vmem, f32[160,2560]{1,0:T(8,128)S(1)} %bitcast.7, f32[10,2560]{1,0:T(8,128)S(1)} %collective-permute-done.top_ref, ...), custom_call_target="tpu_custom_call" | custom-call | tf_op jit(solution)/shard_map/band_planes/pallas_call | solution.py:346
  27.2 0.1 collective-permute-start.2
  27.3 2.3 %collective-permute-done.2 = f32[1600,128]{1,0:T(8,128)S(1)} collective-permute-done((f32[1600,128]{1,0:T(8,128)S(1)}, f32[1600,128]{1,0:T(8,128)S(1)}, u32[]{:S(2)}, u32[]{:S(2)}) %collective-permute-start.2) | collective-permute-done | bytes 819232 | tf_op jit(solution)/shard_map/ppermute | solution.py:377
  29.7 0.1 mul.18
  29.8 5.9 %collective-permute-start.3 = (f32[600,128]{1,0:T(8,128)S(1)}, f32[600,128]{1,0:T(8,128)S(1)}, u32[]{:S(2)}, u32[]{:S(2)}) collective-permute-start(f32[600,128]{1,0:T(8,128)S(1)} %slice.49), channel_id=1, source_target_pairs={{0,224},{16,48},{32,0},{48,80},{64,32},{80,112},{96,64},{112,144},... | collective-permute-start | bytes 921608 | tf_op jit(solution)/shard_map/ppermute | solution.py:372
  35.7 0.1 collective-permute-start.4
  35.8 5.7 %collective-permute-done.3 = f32[600,128]{1,0:T(8,128)S(1)} collective-permute-done((f32[600,128]{1,0:T(8,128)S(1)}, f32[600,128]{1,0:T(8,128)S(1)}, u32[]{:S(2)}, u32[]{:S(2)}) %collective-permute-start.3) | collective-permute-done | bytes 307232 | tf_op jit(solution)/shard_map/ppermute | solution.py:372
  41.6 1.2 %collective-permute-done.4 = f32[400,128]{1,0:T(8,128)S(1)} collective-permute-done((f32[400,128]{1,0:T(8,128)S(1)}, f32[400,128]{1,0:T(8,128)S(1)}, u32[]{:S(2)}, u32[]{:S(2)}) %collective-permute-start.4) | collective-permute-done | bytes 204832 | tf_op jit(solution)/shard_map/ppermute | solution.py:372
  42.8 1.0 %collective-permute-start.5 = (f32[200,128]{1,0:T(8,128)S(1)}, f32[200,128]{1,0:T(8,128)S(1)}, u32[]{:S(2)}, u32[]{:S(2)}) collective-permute-start(f32[200,128]{1,0:T(8,128)S(1)} %get-tuple-element.17), channel_id=1, source_target_pairs={{0,96},{16,176},{32,128},{48,208},{64,160},{80,240},{96,192},{112,... | collective-permute-start | bytes 307208 | tf_op jit(solution)/shard_map/ppermute | solution.py:372
  43.8 1.6 %collective-permute-start.6 = (f32[200,128]{1,0:T(8,128)S(1)}, f32[200,128]{1,0:T(8,128)S(1)}, u32[]{:S(2)}, u32[]{:S(2)}) collective-permute-start(f32[200,128]{1,0:T(8,128)S(1)} %get-tuple-element.18), channel_id=1, source_target_pairs={{0,192},{16,80},{32,224},{48,112},{64,0},{80,144},{96,32},{112,176... | collective-permute-start | bytes 307208 | tf_op jit(solution)/shard_map/ppermute | solution.py:372
  45.5 9.1 %collective-permute-done.5 = f32[200,128]{1,0:T(8,128)S(1)} collective-permute-done((f32[200,128]{1,0:T(8,128)S(1)}, f32[200,128]{1,0:T(8,128)S(1)}, u32[]{:S(2)}, u32[]{:S(2)}) %collective-permute-start.5) | collective-permute-done | bytes 102432 | tf_op jit(solution)/shard_map/ppermute | solution.py:372
  54.6 0.0 collective-permute-done.6
  54.6 0.7 %reshape.5 = f32[5,5,1024]{2,1,0:T(8,128)} reshape(f32[200,128]{1,0:T(8,128)S(1)} %fusion.1) | data formatting | bytes 204800 | tf_op jit(solution)/shard_map/reshape | solution.py:391
  (5 shorter events, 0.1 us)
Async XLA Ops:
  1.0 12.4 %collective-permute-start.1 = (f32[10,2560]{1,0:T(8,128)S(1)}, f32[10,2560]{1,0:T(8,128)S(1)}, u32[]{:S(2)}, u32[]{:S(2)}) collective-permute-start(f32[10,2560]{1,0:T(8,128)S(1)} %get-tuple-element.15), channel_id=1, source_target_pairs={{1,0},{2,1},{3,2},{4,3},{5,4},{6,5},{7,6},{8,7},{9,8},{10,9},{11,1... | collective-permute-start | bytes 307208 | tf_op jit(solution)/shard_map/ppermute | solution.py:389
  6.2 9.7 %collective-permute-start = (f32[10,2560]{1,0:T(8,128)S(1)}, f32[10,2560]{1,0:T(8,128)S(1)}, u32[]{:S(2)}, u32[]{:S(2)}) collective-permute-start(f32[10,2560]{1,0:T(8,128)S(1)} %get-tuple-element.16), channel_id=1, source_target_pairs={{0,1},{1,2},{2,3},{3,4},{4,5},{5,6},{6,7},{7,8},{8,9},{9,10},{10,1... | collective-permute-start | bytes 307208 | tf_op jit(solution)/shard_map/ppermute | solution.py:388
  8.1 7.7 %copy-start = (f32[1,160,2560]{2,1,0:T(8,128)S(1)}, f32[1,160,2560]{2,1,0:T(8,128)}, u32[]{:S(2)}) copy-start(f32[1,160,2560]{2,1,0:T(8,128)} %param.7) | copy-start | bytes 4915204
  27.2 2.4 %collective-permute-start.2 = (f32[1600,128]{1,0:T(8,128)S(1)}, f32[1600,128]{1,0:T(8,128)S(1)}, u32[]{:S(2)}, u32[]{:S(2)}) collective-permute-start(f32[1600,128]{1,0:T(8,128)S(1)} %get-tuple-element.14), channel_id=1, source_target_pairs={{0,16},{16,0},{32,48},{48,32},{64,80},{80,64},{96,112},{112,96},{1... | collective-permute-start | bytes 2457608 | tf_op jit(solution)/shard_map/ppermute | solution.py:377
  29.8 11.8 %collective-permute-start.3 = (f32[600,128]{1,0:T(8,128)S(1)}, f32[600,128]{1,0:T(8,128)S(1)}, u32[]{:S(2)}, u32[]{:S(2)}) collective-permute-start(f32[600,128]{1,0:T(8,128)S(1)} %slice.49), channel_id=1, source_target_pairs={{0,224},{16,48},{32,0},{48,80},{64,32},{80,112},{96,64},{112,144},... | collective-permute-start | bytes 921608 | tf_op jit(solution)/shard_map/ppermute | solution.py:372
  35.7 7.0 %collective-permute-start.4 = (f32[400,128]{1,0:T(8,128)S(1)}, f32[400,128]{1,0:T(8,128)S(1)}, u32[]{:S(2)}, u32[]{:S(2)}) collective-permute-start(f32[400,128]{1,0:T(8,128)S(1)} %slice.51), channel_id=1, source_target_pairs={{0,32},{16,240},{32,64},{48,16},{64,96},{80,48},{96,128},{112,80},... | collective-permute-start | bytes 614408 | tf_op jit(solution)/shard_map/ppermute | solution.py:372
  42.8 11.8 %collective-permute-start.5 = (f32[200,128]{1,0:T(8,128)S(1)}, f32[200,128]{1,0:T(8,128)S(1)}, u32[]{:S(2)}, u32[]{:S(2)}) collective-permute-start(f32[200,128]{1,0:T(8,128)S(1)} %get-tuple-element.17), channel_id=1, source_target_pairs={{0,96},{16,176},{32,128},{48,208},{64,160},{80,240},{96,192},{112,... | collective-permute-start | bytes 307208 | tf_op jit(solution)/shard_map/ppermute | solution.py:372
  43.8 10.7 %collective-permute-start.6 = (f32[200,128]{1,0:T(8,128)S(1)}, f32[200,128]{1,0:T(8,128)S(1)}, u32[]{:S(2)}, u32[]{:S(2)}) collective-permute-start(f32[200,128]{1,0:T(8,128)S(1)} %get-tuple-element.18), channel_id=1, source_target_pairs={{0,192},{16,80},{32,224},{48,112},{64,0},{80,144},{96,32},{112,176... | collective-permute-start | bytes 307208 | tf_op jit(solution)/shard_map/ppermute | solution.py:372

commit v6 on v4

--- a/solution.py
+++ b/solution.py
@@ -373,10 +373,11 @@
 
 def reduced(keep, away):
     size = keep.shape[0] // 8
-    parts = keep * lax.ppermute(away, "sep", [(s, s ^ 1) for s in range(16)])
-    ahead = along_z(parts[3 * size : 5 * size], 1)
-    behind = along_z(parts[5 * size :], -1)
-    near = parts[: 3 * size] * behind
+    across = [(s, s ^ 1) for s in range(16)]
+    far = keep[3 * size :] * lax.ppermute(away[3 * size :], "sep", across)
+    behind = along_z(far[2 * size :], -1)
+    ahead = along_z(far[: 2 * size], 1)
+    near = keep[: 3 * size] * lax.ppermute(away[: 3 * size], "sep", across) * behind
     third = along_z(near[size : 2 * size] * ahead[size:], 3)
     sixth = along_z(near[2 * size :], -2)
     return near[:size] * ahead[:size] * third * sixth

time: 55.5 us -> 55 us (level)
  waiting for transfers between devices: 20.8 us -> 19.6 us
  starting transfers between devices: 15.9 us -> 16.5 us
    ppermute x1 -> x2, waiting for transfers between devices: 2.32 us -> 1.27 us  [the longest x1 1.27 us: reduced(): far = keep[3 * size:] * lax.ppermute(away[3 * size:], 'sep', across)]
    ppermute x1 -> x2, starting transfers between devices: 0.09 us -> 0.67 us  [the longest x1 0.58 us: reduced(): lax.ppermute(away[:3 * size], 'sep', across)]
  transfers between devices with their start and end apart: 7 -> 8, of which waited for: 5 -> 5; matrix products, arithmetic and copies ran while one was open for 0% -> 0% of each run, Pallas kernels for 10% -> 10%
where the time goes in v6:
time: 55 us; the launch traced here: 54.8 us
  waiting for transfers between devices  19.6 us (36%)
  Pallas kernels  16.6 us (30%)
  starting transfers between devices  16.5 us (30%)
  local copies, waits for them, and re-layouts  1.8 us (3%)
    ppermute x4, waiting for transfers between devices, along_z(): return lax.ppermute(array, 'sep', pairs)  15.9 us
    pallas_call x1, Pallas kernels, band_planes(): pl.pallas_call(band_kernel, out_shape=[half, half], in_specs=[hbm, vmem,...  11.3 us
    ppermute x4, starting transfers between devices, along_z(): return lax.ppermute(array, 'sep', pairs)  8.69 us
    pallas_call x1, Pallas kernels, band_planes(): pl.pallas_call(first_kernel, out_shape=[jax.ShapeDtypeStruct((5, windows,...  5.29 us
    ppermute x1, starting transfers between devices, local(): lax.ppermute(second[:HALO], 'tile', [(i + 1, i) for i in range(15)])  5.19 us
    ppermute x1, waiting for transfers between devices, local(): top = lax.ppermute(second[-HALO:], 'tile', [(i, i + 1) for i in range(15)])  2.41 us
    ppermute x1, starting transfers between devices, local(): top = lax.ppermute(second[-HALO:], 'tile', [(i, i + 1) for i in range(15)])  1.92 us
    ppermute x1, waiting for transfers between devices, reduced(): far = keep[3 * size:] * lax.ppermute(away[3 * size:], 'sep', across)  1.27 us
  transfers between devices with their start and end apart: 8, of which 5 were waited for; matrix products, arithmetic and copies ran while one was open for 0% of the time, Pallas kernels for 10%

profile of v6, /device:TPU:6, one launch (start us, length us, event | category | flops | bytes accessed | tf_op | source)
XLA Modules:
  0.0 54.8 jit_solution(12749437276069619130)
XLA Ops:
  0.0 1.0 %slice_bitcast_fusion = (f32[16,2560]{1,0:T(8,128)S(1)}, f32[16,2560]{1,0:T(8,128)S(1)}) fusion(f32[1,160,2560]{2,1,0:T(8,128)} %param.7), kind=kLoop, calls=%fused_computation.2 | loop fusion | bytes 655360 | tf_op jit(solution)/shard_map/slice | solution.py:389
  1.0 5.2 %collective-permute-start.1 = (f32[16,2560]{1,0:T(8,128)S(1)}, f32[16,2560]{1,0:T(8,128)S(1)}, u32[]{:S(2)}, u32[]{:S(2)}) collective-permute-start(f32[16,2560]{1,0:T(8,128)S(1)} %get-tuple-element.15), channel_id=1, source_target_pairs={{1,0},{2,1},{3,2},{4,3},{5,4},{6,5},{7,6},{8,7},{9,8},{10,9},{11,1... | collective-permute-start | bytes 491528 | tf_op jit(solution)/shard_map/ppermute | solution.py:389
  6.2 1.9 %collective-permute-start = (f32[16,2560]{1,0:T(8,128)S(1)}, f32[16,2560]{1,0:T(8,128)S(1)}, u32[]{:S(2)}, u32[]{:S(2)}) collective-permute-start(f32[16,2560]{1,0:T(8,128)S(1)} %get-tuple-element.16), channel_id=1, source_target_pairs={{0,1},{1,2},{2,3},{3,4},{4,5},{5,6},{6,7},{7,8},{8,9},{9,10},{10,1... | collective-permute-start | bytes 491528 | tf_op jit(solution)/shard_map/ppermute | solution.py:388
  8.1 0.0 copy-start
  8.2 5.3 %first_spectra.1 = (f32[5,400,256]{2,1,0:T(8,128)S(1)}, f32[400,128]{1,0:T(8,128)S(1)}, f32[8,8,128]{2,1,0:T(8,128)S(1)}) custom-call(f32[2,5,1,80]{3,2,1,0:T(1,128)} %bitcast.9, f32[160,2560]{1,0:T(8,128)} %first_hbm.1, bf16[5,256,256]{2,1,0:T(8,128)(2,1)} %constant.4.clone.high_hbm, bf16[5,256,256]{2,1,0:T(8,128)(2,1)} %constant.5.clone.low_hbm), custom_call_target="tpu_custom_call" | custom-call | flops 10000000000 | bytes 20000000 | tf_op jit(solution)/shard_map/first_spectra/pallas_call | solution.py:323
  13.5 0.0 collective-permute-done.1.bottom_ref
  13.5 2.4 %collective-permute-done.top_ref = f32[16,2560]{1,0:T(8,128)S(1)} collective-permute-done((f32[16,2560]{1,0:T(8,128)S(1)}, f32[16,2560]{1,0:T(8,128)S(1)}, u32[]{:S(2)}, u32[]{:S(2)}) %collective-permute-start) | collective-permute-done | bytes 163872 | tf_op jit(solution)/shard_map/ppermute | solution.py:388
  15.9 0.0 copy-done
  15.9 11.3 %band_planes.1 = (f32[1600,128]{1,0:T(8,128)S(1)}, f32[1600,128]{1,0:T(8,128)S(1)}) custom-call(s32[2,5,1,80]{3,2,1,0:T(1,128)} %bitcast.8, f32[8,8,128]{2,1,0:T(8,128)S(1)} %get-tuple-element.10.taps_vmem, f32[160,2560]{1,0:T(8,128)S(1)} %bitcast.7, f32[16,2560]{1,0:T(8,128)S(1)} %collective-permute-done.top_ref, ...), custom_call_target="tpu_custom_call" | custom-call | tf_op jit(solution)/shard_map/band_planes/pallas_call | solution.py:345
  27.3 0.1 collective-permute-start.3
  27.4 0.6 %collective-permute-start.2 = (f32[600,128]{1,0:T(8,128)S(1)}, f32[600,128]{1,0:T(8,128)S(1)}, u32[]{:S(2)}, u32[]{:S(2)}) collective-permute-start(f32[600,128]{1,0:T(8,128)S(1)} %slice.50), channel_id=1, source_target_pairs={{0,16},{16,0},{32,48},{48,32},{64,80},{80,64},{96,112},{112,96},{1... | collective-permute-start | bytes 921608 | tf_op jit(solution)/shard_map/ppermute | solution.py:380
  28.0 1.3 %collective-permute-done.3 = f32[1000,128]{1,0:T(8,128)S(1)} collective-permute-done((f32[1000,128]{1,0:T(8,128)S(1)}, f32[1000,128]{1,0:T(8,128)S(1)}, u32[]{:S(2)}, u32[]{:S(2)}) %collective-permute-start.3) | collective-permute-done | bytes 512032 | tf_op jit(solution)/shard_map/ppermute | solution.py:377
  29.3 0.1 slice_multiply_fusion
  29.3 5.9 %collective-permute-start.4 = (f32[600,128]{1,0:T(8,128)S(1)}, f32[600,128]{1,0:T(8,128)S(1)}, u32[]{:S(2)}, u32[]{:S(2)}) collective-permute-start(f32[600,128]{1,0:T(8,128)S(1)} %slice.60), channel_id=1, source_target_pairs={{0,224},{16,48},{32,0},{48,80},{64,32},{80,112},{96,64},{112,144},... | collective-permute-start | bytes 921608 | tf_op jit(solution)/shard_map/ppermute | solution.py:371
  35.3 0.1 collective-permute-start.5
  35.4 0.0 collective-permute-done.2
  35.4 5.7 %collective-permute-done.4 = f32[600,128]{1,0:T(8,128)S(1)} collective-permute-done((f32[600,128]{1,0:T(8,128)S(1)}, f32[600,128]{1,0:T(8,128)S(1)}, u32[]{:S(2)}, u32[]{:S(2)}) %collective-permute-start.4) | collective-permute-done | bytes 307232 | tf_op jit(solution)/shard_map/ppermute | solution.py:371
  41.1 0.1 multiply_multiply_fusion
  41.2 1.2 %collective-permute-done.5 = f32[400,128]{1,0:T(8,128)S(1)} collective-permute-done((f32[400,128]{1,0:T(8,128)S(1)}, f32[400,128]{1,0:T(8,128)S(1)}, u32[]{:S(2)}, u32[]{:S(2)}) %collective-permute-start.5) | collective-permute-done | bytes 204832 | tf_op jit(solution)/shard_map/ppermute | solution.py:371
  42.4 1.0 %collective-permute-start.6 = (f32[200,128]{1,0:T(8,128)S(1)}, f32[200,128]{1,0:T(8,128)S(1)}, u32[]{:S(2)}, u32[]{:S(2)}) collective-permute-start(f32[200,128]{1,0:T(8,128)S(1)} %get-tuple-element.17), channel_id=1, source_target_pairs={{0,96},{16,176},{32,128},{48,208},{64,160},{80,240},{96,192},{112,... | collective-permute-start | bytes 307208 | tf_op jit(solution)/shard_map/ppermute | solution.py:371
  43.4 1.6 %collective-permute-start.7 = (f32[200,128]{1,0:T(8,128)S(1)}, f32[200,128]{1,0:T(8,128)S(1)}, u32[]{:S(2)}, u32[]{:S(2)}) collective-permute-start(f32[200,128]{1,0:T(8,128)S(1)} %get-tuple-element.18), channel_id=1, source_target_pairs={{0,192},{16,80},{32,224},{48,112},{64,0},{80,144},{96,32},{112,176... | collective-permute-start | bytes 307208 | tf_op jit(solution)/shard_map/ppermute | solution.py:371
  45.0 9.1 %collective-permute-done.6 = f32[200,128]{1,0:T(8,128)S(1)} collective-permute-done((f32[200,128]{1,0:T(8,128)S(1)}, f32[200,128]{1,0:T(8,128)S(1)}, u32[]{:S(2)}, u32[]{:S(2)}) %collective-permute-start.6) | collective-permute-done | bytes 102432 | tf_op jit(solution)/shard_map/ppermute | solution.py:371
  54.1 0.0 collective-permute-done.7
  54.1 0.7 %reshape.5 = f32[5,5,1024]{2,1,0:T(8,128)} reshape(f32[200,128]{1,0:T(8,128)S(1)} %fusion.1) | data formatting | bytes 204800 | tf_op jit(solution)/shard_map/reshape | solution.py:391
  (6 shorter events, 0.1 us)
Async XLA Ops:
  1.0 12.4 %collective-permute-start.1 = (f32[16,2560]{1,0:T(8,128)S(1)}, f32[16,2560]{1,0:T(8,128)S(1)}, u32[]{:S(2)}, u32[]{:S(2)}) collective-permute-start(f32[16,2560]{1,0:T(8,128)S(1)} %get-tuple-element.15), channel_id=1, source_target_pairs={{1,0},{2,1},{3,2},{4,3},{5,4},{6,5},{7,6},{8,7},{9,8},{10,9},{11,1... | collective-permute-start | bytes 491528 | tf_op jit(solution)/shard_map/ppermute | solution.py:389
  6.2 9.7 %collective-permute-start = (f32[16,2560]{1,0:T(8,128)S(1)}, f32[16,2560]{1,0:T(8,128)S(1)}, u32[]{:S(2)}, u32[]{:S(2)}) collective-permute-start(f32[16,2560]{1,0:T(8,128)S(1)} %get-tuple-element.16), channel_id=1, source_target_pairs={{0,1},{1,2},{2,3},{3,4},{4,5},{5,6},{6,7},{7,8},{8,9},{9,10},{10,1... | collective-permute-start | bytes 491528 | tf_op jit(solution)/shard_map/ppermute | solution.py:388
  8.1 7.7 %copy-start = (f32[1,160,2560]{2,1,0:T(8,128)S(1)}, f32[1,160,2560]{2,1,0:T(8,128)}, u32[]{:S(2)}) copy-start(f32[1,160,2560]{2,1,0:T(8,128)} %param.7) | copy-start | bytes 4915204
  27.3 2.0 %collective-permute-start.3 = (f32[1000,128]{1,0:T(8,128)S(1)}, f32[1000,128]{1,0:T(8,128)S(1)}, u32[]{:S(2)}, u32[]{:S(2)}) collective-permute-start(f32[1000,128]{1,0:T(8,128)S(1)} %slice.52), channel_id=1, source_target_pairs={{0,16},{16,0},{32,48},{48,32},{64,80},{80,64},{96,112},{112,96},{1... | collective-permute-start | bytes 1536008 | tf_op jit(solution)/shard_map/ppermute | solution.py:377
  27.4 8.0 %collective-permute-start.2 = (f32[600,128]{1,0:T(8,128)S(1)}, f32[600,128]{1,0:T(8,128)S(1)}, u32[]{:S(2)}, u32[]{:S(2)}) collective-permute-start(f32[600,128]{1,0:T(8,128)S(1)} %slice.50), channel_id=1, source_target_pairs={{0,16},{16,0},{32,48},{48,32},{64,80},{80,64},{96,112},{112,96},{1... | collective-permute-start | bytes 921608 | tf_op jit(solution)/shard_map/ppermute | solution.py:380
  29.3 11.8 %collective-permute-start.4 = (f32[600,128]{1,0:T(8,128)S(1)}, f32[600,128]{1,0:T(8,128)S(1)}, u32[]{:S(2)}, u32[]{:S(2)}) collective-permute-start(f32[600,128]{1,0:T(8,128)S(1)} %slice.60), channel_id=1, source_target_pairs={{0,224},{16,48},{32,0},{48,80},{64,32},{80,112},{96,64},{112,144},... | collective-permute-start | bytes 921608 | tf_op jit(solution)/shard_map/ppermute | solution.py:371
  35.3 7.0 %collective-permute-start.5 = (f32[400,128]{1,0:T(8,128)S(1)}, f32[400,128]{1,0:T(8,128)S(1)}, u32[]{:S(2)}, u32[]{:S(2)}) collective-permute-start(f32[400,128]{1,0:T(8,128)S(1)} %slice.62), channel_id=1, source_target_pairs={{0,32},{16,240},{32,64},{48,16},{64,96},{80,48},{96,128},{112,80},... | collective-permute-start | bytes 614408 | tf_op jit(solution)/shard_map/ppermute | solution.py:371
  42.4 11.7 %collective-permute-start.6 = (f32[200,128]{1,0:T(8,128)S(1)}, f32[200,128]{1,0:T(8,128)S(1)}, u32[]{:S(2)}, u32[]{:S(2)}) collective-permute-start(f32[200,128]{1,0:T(8,128)S(1)} %get-tuple-element.17), channel_id=1, source_target_pairs={{0,96},{16,176},{32,128},{48,208},{64,160},{80,240},{96,192},{112,... | collective-permute-start | bytes 307208 | tf_op jit(solution)/shard_map/ppermute | solution.py:371
  43.4 10.7 %collective-permute-start.7 = (f32[200,128]{1,0:T(8,128)S(1)}, f32[200,128]{1,0:T(8,128)S(1)}, u32[]{:S(2)}, u32[]{:S(2)}) collective-permute-start(f32[200,128]{1,0:T(8,128)S(1)} %get-tuple-element.18), channel_id=1, source_target_pairs={{0,192},{16,80},{32,224},{48,112},{64,0},{80,144},{96,32},{112,176... | collective-permute-start | bytes 307208 | tf_op jit(solution)/shard_map/ppermute | solution.py:371
